TPU v7x, 128 devices: a whole 4x4x4 slice. The times are simulated.
128 devices in a mesh: fsdp: 32 (over z, x_hi, y), tensor: 4 (over x_lo, core).
Axes of the slice: x: 4 (x_hi: 2, x_lo: 2; x = x_hi * 2 + x_lo), y: 4, z: 4, core: 2. Of those that a mesh axis runs over, the one named last changes fastest.
Arguments:
- tokens: bfloat16 [512, 32, 2048], P('tensor', 'fsdp'), may hold values from -6 to 6
- attend_gain: bfloat16 [2048], P('fsdp'), may hold values from 0.5 to 1.5
- joint_weight: bfloat16 [2048, 4096], P('fsdp', 'tensor'), may hold values from -0.125 to 0.125
- mixing_weight: bfloat16 [2048, 2048], P('tensor', 'fsdp'), may hold values from -0.75 to 0.75
- feed_gain: bfloat16 [2048], P('fsdp'), may hold values from 0.5 to 1.5
- gate_weight: bfloat16 [2048, 8192], P('fsdp', 'tensor'), may hold values from -0.125 to 0.125
- up_weight: bfloat16 [2048, 8192], P('fsdp', 'tensor'), may hold values from -0.125 to 0.125
- down_weight: bfloat16 [8192, 2048], P('tensor', 'fsdp'), may hold values from -0.0625 to 0.0625
- lengths: int32 [32, 7], P('fsdp'), may hold values from 1 to 256, 512 in all within a row
- parents: int32 [32, 7], P('fsdp'), may hold values from 0 to 5, as said below
- cotangent: float32 [512, 32, 2048], P('tensor', 'fsdp'), may hold values from -6 to 6
Outputs:
- layer_output: float32 [512, 32, 2048], P('tensor', 'fsdp')
- input_gradient: float32 [512, 32, 2048], P('tensor', 'fsdp')
- attend_gradient: float32 [2048], P('fsdp')
- joint_gradient: float32 [2048, 4096], P('fsdp', 'tensor')
- mixing_gradient: float32 [2048, 2048], P('tensor', 'fsdp')
- feed_gradient: float32 [2048], P('fsdp')
- gate_gradient: float32 [2048, 8192], P('fsdp', 'tensor')
- up_gradient: float32 [2048, 8192], P('fsdp', 'tensor')
- down_gradient: float32 [8192, 2048], P('tensor', 'fsdp')
Inputs may be any that keep to these rules, and one draw needn't show every extreme that they name: `lengths`: each row sums to 512, and every row's largest entry is 256. `parents`: entry s >= 1 of a row is a segment number below s; entry 0 is 0.
All inputs are finite; a program needn't handle non-finite values.
Results may differ from a plain program's by a relative error of at most 0.028.
Values may be sent and summed in bfloat16 or wider, within the bound.
No kernel may reach another device: no remote copies, remote signals or barrier semaphores. Data moves between devices by JAX's collectives and lax.ppermute only.
A program may use at most 192 MiB of HBM per device.

v0:
```python
import math

import jax
import jax.numpy as jnp
from jax import lax
from jax.sharding import PartitionSpec as P

HEADS = 16
KVH = 8
HD = 128


EPSILON = 1e-06
ROPE_BASE = 1000000.0
NEGATIVE = -1e30


def tree_layout(lengths, parents, count):
    nseg = lengths.shape[1]
    batch = lengths.shape[0]
    ends = jnp.cumsum(lengths, axis=1)
    starts = ends - lengths
    place = jnp.arange(count, dtype=jnp.int32)
    segment = jnp.sum((place[:, None, None] >= ends[None, :, : nseg - 1]).astype(jnp.int32), axis=2)
    order = jnp.arange(nseg, dtype=jnp.int32)
    rows = [(order == 0).astype(jnp.float32)[None, :] * jnp.ones((batch, 1), jnp.float32)]
    depth = [jnp.zeros((batch,), jnp.int32)]
    for later in range(1, nseg):
        above = jnp.zeros_like(rows[0])
        reach = jnp.zeros_like(depth[0])
        for earlier in range(later):
            hit = parents[:, later] == earlier
            above = above + hit.astype(jnp.float32)[:, None] * rows[earlier]
            reach = reach + jnp.where(hit, depth[earlier] + lengths[:, earlier], 0)
        rows.append(above + (order == later).astype(jnp.float32)[None, :])
        depth.append(reach)
    ancestry = jnp.stack(rows, axis=1)
    begin = jnp.stack(depth, axis=1)
    pick = (segment[:, :, None] == order[None, None, :]).astype(jnp.float32)
    shift = (begin - starts).astype(jnp.float32)
    position = place[:, None].astype(jnp.float32) + jnp.sum(pick * shift[None], axis=2)
    linked = jnp.einsum("ibs,bst,jbt->bij", pick, ancestry, pick)
    causal = place[None, :] <= place[:, None]
    return (position, (linked > 0.5) & causal[None])


def rotary_tables(position, width):
    half = width // 2
    rates = jnp.exp(jnp.arange(half, dtype=jnp.float32) * (-2.0 * math.log(ROPE_BASE) / width))
    angle = position[..., None] * rates
    return (jnp.cos(angle), jnp.sin(angle))


def rotate(values, cosine, sine):
    half = values.shape[-1] // 2
    shape = cosine.shape[:-1] + (1,) * (values.ndim - cosine.ndim) + cosine.shape[-1:]
    cosine = cosine.reshape(shape)
    sine = sine.reshape(shape)
    first = values[..., :half]
    second = values[..., half:]
    return jnp.concatenate(
        [first * cosine - second * sine, second * cosine + first * sine], axis=-1
    )


def norm_back(slope, incoming, scale, gain):
    weighted = slope * gain
    gain_part = jnp.sum(slope * incoming * scale, axis=(0, 1))
    cubed = scale * scale * scale
    back = scale * weighted - incoming * cubed * jnp.mean(
        weighted * incoming, axis=2, keepdims=True
    )
    return (back, gain_part)


def shards(
    tokens,
    attend_gain,
    joint_weight,
    mixing_weight,
    feed_gain,
    gate_weight,
    up_weight,
    down_weight,
    lengths,
    parents,
    cotangent,
):
    groups = HEADS // KVH
    factor = 1.0 / math.sqrt(HD)
    incoming = tokens.astype(jnp.float32)
    local_rows = tokens.shape[0]
    count = local_rows * lax.axis_size("tensor")
    trees = tokens.shape[1]
    position, allowed = tree_layout(lengths, parents, count)
    cosine, sine = rotary_tables(position, HD)
    mask_wide = allowed[:, None, None]
    joint_full, mixing_full, gain_one = (
        lax.all_gather(joint_weight, "fsdp", axis=0, tiled=True),
        lax.all_gather(mixing_weight, "fsdp", axis=1, tiled=True),
        lax.all_gather(attend_gain, "fsdp", axis=0, tiled=True),
    )
    scale_one = lax.rsqrt(jnp.mean(incoming * incoming, axis=2, keepdims=True) + EPSILON)
    normed_one = (incoming * scale_one * gain_one.astype(jnp.float32)).astype(jnp.bfloat16)
    normed_all = lax.all_gather(normed_one, "tensor", axis=0, tiled=True)
    joint = jnp.einsum("lbd,de->lbe", normed_all, joint_full, preferred_element_type=jnp.float32)
    kv_local = joint.shape[2] // ((groups + 2) * HD)
    joint = joint.reshape(count, trees, kv_local, groups + 2, HD)
    queries = rotate(joint[:, :, :, :groups], cosine, sine).astype(jnp.bfloat16)
    keys = rotate(joint[:, :, :, groups], cosine, sine).astype(jnp.bfloat16)
    values = joint[:, :, :, groups + 1].astype(jnp.bfloat16)
    scores = (
        jnp.einsum("ibkgd,jbkd->bkgij", queries, keys, preferred_element_type=jnp.float32) * factor
    )
    masked = jnp.where(mask_wide, scores, NEGATIVE)
    highest = jnp.max(masked, axis=-1, keepdims=True)
    powers = jnp.exp(masked - highest)
    total = jnp.sum(powers, axis=-1, keepdims=True)
    chance_low = (powers / total).astype(jnp.bfloat16)
    logsum = highest + jnp.log(total)
    mixed = jnp.einsum("bkgij,jbkd->ibkgd", chance_low, values, preferred_element_type=jnp.float32)
    mixed = mixed.reshape(count, trees, kv_local * groups * HD).astype(jnp.bfloat16)
    rows = mixed
    middle = incoming + lax.psum_scatter(
        jnp.einsum("lbe,ed->lbd", rows, mixing_full, preferred_element_type=jnp.float32),
        "tensor",
        scatter_dimension=0,
        tiled=True,
    )
    gate_full, up_full, down_full, gain_two = (
        lax.all_gather(gate_weight, "fsdp", axis=0, tiled=True),
        lax.all_gather(up_weight, "fsdp", axis=0, tiled=True),
        lax.all_gather(down_weight, "fsdp", axis=1, tiled=True),
        lax.all_gather(feed_gain, "fsdp", axis=0, tiled=True),
    )
    scale_two = lax.rsqrt(jnp.mean(middle * middle, axis=2, keepdims=True) + EPSILON)
    normed_two = (middle * scale_two * gain_two.astype(jnp.float32)).astype(jnp.bfloat16)
    normed_two_all = lax.all_gather(normed_two, "tensor", axis=0, tiled=True)
    gate = jnp.einsum("lbd,df->lbf", normed_two_all, gate_full, preferred_element_type=jnp.float32)
    upper = jnp.einsum("lbd,df->lbf", normed_two_all, up_full, preferred_element_type=jnp.float32)
    sigma = jax.nn.sigmoid(gate)
    hidden = (gate * sigma * upper).astype(jnp.bfloat16)
    rows = hidden
    layer_output = middle + lax.psum_scatter(
        jnp.einsum("lbf,fd->lbd", rows, down_full, preferred_element_type=jnp.float32).astype(
            jnp.bfloat16
        ),
        "tensor",
        scatter_dimension=0,
        tiled=True,
    ).astype(jnp.float32)
    joint_full, mixing_full, gain_one, gate_full, up_full, down_full, gain_two = (
        lax.all_gather(joint_weight, "fsdp", axis=0, tiled=True),
        lax.all_gather(mixing_weight, "fsdp", axis=1, tiled=True),
        lax.all_gather(attend_gain, "fsdp", axis=0, tiled=True),
        lax.all_gather(gate_weight, "fsdp", axis=0, tiled=True),
        lax.all_gather(up_weight, "fsdp", axis=0, tiled=True),
        lax.all_gather(down_weight, "fsdp", axis=1, tiled=True),
        lax.all_gather(feed_gain, "fsdp", axis=0, tiled=True),
    )
    feed_all = lax.all_gather(cotangent.astype(jnp.bfloat16), "tensor", axis=0, tiled=True)
    down_grad = jnp.einsum("lbf,lbd->fd", hidden, feed_all, preferred_element_type=jnp.float32)
    hidden_slope = jnp.einsum(
        "lbd,fd->lbf", feed_all, down_full, preferred_element_type=jnp.float32
    )
    gate_slope = (hidden_slope * upper * sigma * (1.0 + gate * (1.0 - sigma))).astype(jnp.bfloat16)
    upper_slope = (hidden_slope * gate * sigma).astype(jnp.bfloat16)
    gate_grad = jnp.einsum(
        "lbd,lbf->df", normed_two_all, gate_slope, preferred_element_type=jnp.float32
    )
    upper_grad = jnp.einsum(
        "lbd,lbf->df", normed_two_all, upper_slope, preferred_element_type=jnp.float32
    )
    normed_two_slope = lax.psum_scatter(
        jnp.einsum("lbf,df->lbd", gate_slope, gate_full, preferred_element_type=jnp.float32)
        + jnp.einsum("lbf,df->lbd", upper_slope, up_full, preferred_element_type=jnp.float32),
        "tensor",
        scatter_dimension=0,
        tiled=True,
    )
    middle_back, feed_gain_part = norm_back(
        normed_two_slope, middle, scale_two, gain_two.astype(jnp.float32)
    )
    middle_slope = cotangent + middle_back
    gate_sum, upper_sum, down_sum, feed_gain_sum = (
        lax.psum_scatter(
            gate_grad.astype(jnp.bfloat16), "fsdp", scatter_dimension=0, tiled=True
        ).astype(jnp.float32),
        lax.psum_scatter(
            upper_grad.astype(jnp.bfloat16), "fsdp", scatter_dimension=0, tiled=True
        ).astype(jnp.float32),
        lax.psum_scatter(
            down_grad.astype(jnp.bfloat16), "fsdp", scatter_dimension=1, tiled=True
        ).astype(jnp.float32),
        lax.psum_scatter(
            feed_gain_part.astype(jnp.bfloat16), "fsdp", scatter_dimension=0, tiled=True
        ).astype(jnp.float32),
    )
    branch_all = lax.all_gather(middle_slope.astype(jnp.bfloat16), "tensor", axis=0, tiled=True)
    mixing_grad = jnp.einsum("lbe,lbd->ed", mixed, branch_all, preferred_element_type=jnp.float32)
    mixed_slope = jnp.einsum(
        "lbd,ed->lbe", branch_all, mixing_full, preferred_element_type=jnp.float32
    )
    mixed_slope = mixed_slope.astype(jnp.bfloat16).reshape(count, trees, kv_local, groups, HD)
    again_scores = (
        jnp.einsum("ibkgd,jbkd->bkgij", queries, keys, preferred_element_type=jnp.float32) * factor
    )
    chance = jnp.exp(jnp.where(mask_wide, again_scores, NEGATIVE) - logsum)
    chance_again = chance.astype(jnp.bfloat16)
    value_slope = jnp.einsum(
        "bkgij,ibkgd->jbkd", chance_again, mixed_slope, preferred_element_type=jnp.float32
    )
    chance_slope = jnp.einsum(
        "ibkgd,jbkd->bkgij", mixed_slope, values, preferred_element_type=jnp.float32
    )
    balance = jnp.sum(chance * chance_slope, axis=-1, keepdims=True)
    score_slope = (chance * (chance_slope - balance)).astype(jnp.bfloat16)
    query_slope = (
        jnp.einsum("bkgij,jbkd->ibkgd", score_slope, keys, preferred_element_type=jnp.float32)
        * factor
    )
    key_slope = (
        jnp.einsum("bkgij,ibkgd->jbkd", score_slope, queries, preferred_element_type=jnp.float32)
        * factor
    )
    query_slope = rotate(query_slope, cosine, -sine)
    key_slope = rotate(key_slope, cosine, -sine)
    joint_slope = jnp.concatenate(
        [query_slope, key_slope[:, :, :, None], value_slope[:, :, :, None]], axis=3
    )
    joint_slope = joint_slope.reshape(count, trees, kv_local * (groups + 2) * HD).astype(
        jnp.bfloat16
    )
    joint_grad = jnp.einsum(
        "lbd,lbe->de", normed_all, joint_slope, preferred_element_type=jnp.float32
    )
    rows = joint_slope
    normed_one_slope = lax.psum_scatter(
        jnp.einsum("lbe,de->lbd", rows, joint_full, preferred_element_type=jnp.float32).astype(
            jnp.bfloat16
        ),
        "tensor",
        scatter_dimension=0,
        tiled=True,
    ).astype(jnp.float32)
    incoming_back, attend_gain_part = norm_back(
        normed_one_slope, incoming, scale_one, gain_one.astype(jnp.float32)
    )
    input_gradient = middle_slope + incoming_back
    joint_sum, mixing_sum, attend_gain_sum = (
        lax.psum_scatter(
            joint_grad.astype(jnp.bfloat16), "fsdp", scatter_dimension=0, tiled=True
        ).astype(jnp.float32),
        lax.psum_scatter(
            mixing_grad.astype(jnp.bfloat16), "fsdp", scatter_dimension=1, tiled=True
        ).astype(jnp.float32),
        lax.psum_scatter(
            attend_gain_part.astype(jnp.bfloat16), "fsdp", scatter_dimension=0, tiled=True
        ).astype(jnp.float32),
    )
    attend_total, feed_total = lax.psum((attend_gain_sum, feed_gain_sum), "tensor")
    return (
        layer_output,
        input_gradient,
        attend_total,
        joint_sum,
        mixing_sum,
        feed_total,
        gate_sum,
        upper_sum,
        down_sum,
    )


def solution(mesh):
    in_specs = (
        P("tensor", "fsdp", None),
        P("fsdp"),
        P("fsdp", "tensor"),
        P("tensor", "fsdp"),
        P("fsdp"),
        P("fsdp", "tensor"),
        P("fsdp", "tensor"),
        P("tensor", "fsdp"),
        P("fsdp", None),
        P("fsdp", None),
        P("tensor", "fsdp", None),
    )
    out_specs = (
        P("tensor", "fsdp", None),
        P("tensor", "fsdp", None),
        P("fsdp"),
        P("fsdp", "tensor"),
        P("tensor", "fsdp"),
        P("fsdp"),
        P("fsdp", "tensor"),
        P("fsdp", "tensor"),
        P("tensor", "fsdp"),
    )
    return jax.shard_map(shards, mesh=mesh, in_specs=in_specs, out_specs=out_specs, check_vma=False)
```

profile of v0, /device:TPU:0, one launch (start us, length us, event | category | flops | bytes accessed | tf_op | source)
XLA Modules:
  0.0 1817.2 jit_solution(1048825617326466561)
XLA Ops:
  11.7 99.9 %all-reduce.6 = (bf16[2048]{0:T(1024)(128)(2,1)S(1)}, bf16[2048]{0:T(1024)(128)(2,1)S(1)}) all-reduce(bf16[2048]{0:T(1024)(128)(2,1)S(1)} %dynamic-update-slice, bf16[2048]{0:T(1024)(128)(2,1)S(1)} %dynamic-update-slice.1), channel_id=1, replica_groups=mesh['fsdp'=32,'tensor'=4] {'fsdp'}, use_global_device_ids=true, to_apply=%add | all-reduce | flops 4096 | bytes 16384
  143.0 6.5 copy.63
  149.5 5.2 fusion.29
  159.0 55.0 %all-gather.14.cloned.1.call-done = bf16[512,2048]{0,1:T(8,128)(2,1)} async-done(((bf16[512,64]{0,1:T(8,128)(2,1)}), bf16[512,2048]{0,1:T(8,128)(2,1)}) %all-gather.14.cloned.1.call-update) | async-done | bytes 2097168 | tf_op jit(solution)/shard_map/all_gather | solution.py:100
  213.9 4.9 convolution_bitcast_fusion
  219.5 43.0 %reduce-scatter.10.cloned.1.call-done = f32[128,1,2048]{2,0,1:T(8,128)} async-done(((f32[512,1,2048]{2,0,1:T(8,128)}), f32[128,1,2048]{2,0,1:T(8,128)}) %reduce-scatter.10.cloned.1.call-update) | async-done | bytes 1048592 | tf_op jit(solution)/shard_map/reduce_scatter | solution.py:124
  269.0 101.9 %all-gather.20.cloned.1.call-done = bf16[2048,2048]{1,0:T(8,128)(2,1)} async-done(((bf16[64,2048]{1,0:T(8,128)(2,1)}), bf16[2048,2048]{1,0:T(8,128)(2,1)}) %all-gather.20.cloned.1.call-update) | async-done | bytes 8388624 | tf_op jit(solution)/shard_map/all_gather | solution.py:132
  370.9 29.1 %all-gather.16.cloned.1.call-done = bf16[512,1,2048]{2,0,1:T(8,128)(2,1)} async-done(((bf16[128,1,2048]{2,0,1:T(8,128)(2,1)}), bf16[512,1,2048]{2,0,1:T(8,128)(2,1)}) %all-gather.16.cloned.1.call-update) | async-done | bytes 2097168 | tf_op jit(solution)/shard_map/all_gather | solution.py:138
  400.0 10.5 fusion.21
  410.5 98.1 %all-gather.18.cloned.1.call-done = bf16[2048,2048]{1,0:T(8,128)(2,1)} async-done(((bf16[64,2048]{1,0:T(8,128)(2,1)}), bf16[2048,2048]{1,0:T(8,128)(2,1)}) %all-gather.18.cloned.1.call-update) | async-done | bytes 8388624 | tf_op jit(solution)/shard_map/all_gather | solution.py:131
  508.6 10.6 fusion.23
  519.1 18.7 %all-gather.24.cloned.1.call-done = bf16[512,1,2048]{2,0,1:T(8,128)(2,1)} async-done(((bf16[128,1,2048]{2,0,1:T(8,128)(2,1)}), bf16[512,1,2048]{2,0,1:T(8,128)(2,1)}) %all-gather.24.cloned.1.call-update) | async-done | bytes 2097168 | tf_op jit(solution)/shard_map/all_gather | solution.py:161
  537.8 108.6 %all-gather.22.cloned.1.call-done = bf16[2048,2048]{0,1:T(8,128)(2,1)} async-done(((bf16[2048,64]{0,1:T(8,128)(2,1)}), bf16[2048,2048]{0,1:T(8,128)(2,1)}) %all-gather.22.cloned.1.call-update) | async-done | bytes 8388624 | tf_op jit(solution)/shard_map/all_gather | solution.py:133
  646.4 13.7 multiply_convert_fusion
  660.1 5.0 fusion.95
  665.1 9.5 add_bitcast_fusion
  674.7 9.9 fusion.5
  684.6 33.4 %reduce-scatter.14.cloned.1.call-done = f32[128,1,2048]{2,0,1:T(8,128)} async-done(((f32[512,1,2048]{2,0,1:T(8,128)}), f32[128,1,2048]{2,0,1:T(8,128)}) %reduce-scatter.14.cloned.1.call-update) | async-done | bytes 1048592 | tf_op jit(solution)/shard_map/reduce_scatter | solution.py:174
  720.7 29.0 %reduce-scatter.12.cloned.1.call-done = bf16[128,1,2048]{2,0,1:T(8,128)(2,1)} async-done(((bf16[512,1,2048]{2,0,1:T(8,128)(2,1)}), bf16[128,1,2048]{2,0,1:T(8,128)(2,1)}) %reduce-scatter.12.cloned.1.call-update) | async-done | bytes 524304 | tf_op jit(solution)/shard_map/reduce_scatter | solution.py:144
  754.2 29.1 %all-gather.26.cloned.1.call-done = bf16[512,1,2048]{2,0,1:T(8,128)(2,1)} async-done(((bf16[128,1,2048]{2,0,1:T(8,128)(2,1)}), bf16[512,1,2048]{2,0,1:T(8,128)(2,1)}) %all-gather.26.cloned.1.call-update) | async-done | bytes 2097168 | tf_op jit(solution)/shard_map/all_gather | solution.py:199
  797.9 4.2 convolution_convert_fusion.5
  802.4 10.1 convolution_convert_fusion.1
  812.5 10.1 convolution_convert_fusion.2
  822.9 10.1 convolution_convert_fusion
  833.1 6.0 convolution_convert_fusion.3
  847.3 170.3 %reduce-scatter.20.cloned.1.call-done = bf16[512,64]{0,1:T(8,128)(2,1)} async-done(((bf16[512,2048]{0,1:T(8,128)(2,1)}), bf16[512,64]{0,1:T(8,128)(2,1)}) %reduce-scatter.20.cloned.1.call-update) | async-done | bytes 65552 | tf_op jit(solution)/shard_map/reduce_scatter | solution.py:254
  1019.1 91.0 %all-reduce.5 = (bf16[2048]{0:T(1024)(128)(2,1)S(1)}, bf16[2048]{0:T(1024)(128)(2,1)S(1)}) all-reduce(bf16[2048]{0:T(1024)(128)(2,1)S(1)} %get-tuple-element.47, bf16[2048]{0:T(1024)(128)(2,1)S(1)} %copy-done.14), channel_id=6, replica_groups=mesh['fsdp'=32,'tensor'=4] {'fsdp'}, use_global_device_ids=true, to_apply=%region_15.16.clone | all-reduce | flops 4096 | bytes 16384
  1110.2 6.6 all-reduce.4
  1116.8 101.7 %reduce-scatter.24.cloned.1.call-done = bf16[64,2048]{1,0:T(8,128)(2,1)} async-done(((bf16[2048,2048]{1,0:T(8,128)(2,1)}), bf16[64,2048]{1,0:T(8,128)(2,1)}) %reduce-scatter.24.cloned.1.call-update) | async-done | bytes 262160 | tf_op jit(solution)/shard_map/reduce_scatter | solution.py:189
  1220.3 198.5 %reduce-scatter.22.cloned.1.call-done = bf16[64,2048]{1,0:T(8,128)(2,1)} async-done(((bf16[2048,2048]{1,0:T(8,128)(2,1)}), bf16[64,2048]{1,0:T(8,128)(2,1)}) %reduce-scatter.22.cloned.1.call-update) | async-done | bytes 262160 | tf_op jit(solution)/shard_map/reduce_scatter | solution.py:186
  1420.6 198.1 %reduce-scatter.26.cloned.1.call-done = bf16[2048,64]{0,1:T(8,128)(2,1)} async-done(((bf16[2048,2048]{0,1:T(8,128)(2,1)}), bf16[2048,64]{0,1:T(8,128)(2,1)}) %reduce-scatter.26.cloned.1.call-update) | async-done | bytes 262160 | tf_op jit(solution)/shard_map/reduce_scatter | solution.py:192
  1620.5 187.8 %reduce-scatter.18.cloned.1.call-done = bf16[64,1024]{1,0:T(8,128)(2,1)} async-done(((bf16[2048,1024]{1,0:T(8,128)(2,1)}), bf16[64,1024]{1,0:T(8,128)(2,1)}) %reduce-scatter.18.cloned.1.call-update) | async-done | bytes 131088 | tf_op jit(solution)/shard_map/reduce_scatter | solution.py:251
  (150 shorter events, 64.2 us)
Async XLA Ops:
  7.2 135.1 %copy-start.13 = (s32[1,7]{1,0:T(1,128)S(1)}, s32[1,7]{1,0:T(1,128)}, u32[]{:S(2)}) copy-start(s32[1,7]{1,0:T(1,128)} %param.19) | copy-start | bytes 88
  7.2 135.8 %all-gather.12.cloned.1.call-start = ((), (), s32[]{:S(2)}) async-start(), calls=%async_computation.10 | async-start | bytes 4325376 | tf_op jit(solution)/shard_map/all_gather | solution.py:99
  7.9 141.6 %all-gather.10.cloned.1.call-start = ((), (), s32[]{:S(2)}) async-start(), calls=%async_computation.9 | async-start | bytes 2621440 | tf_op jit(solution)/shard_map/all_gather | solution.py:105
  116.0 97.9 %all-gather.14.cloned.1.call-start = ((), (), s32[]{:S(2)}) async-start(), calls=%async_computation.11 | async-start | bytes 2162688 | tf_op jit(solution)/shard_map/all_gather | solution.py:100
  116.7 145.8 %reduce-scatter.10.cloned.1.call-start = ((), (), s32[]{:S(2)}) async-start(), calls=%async_computation.12 | async-start | bytes 5242880 | tf_op jit(solution)/shard_map/reduce_scatter | solution.py:124
  158.9 59.9 %copy-start.20 = (bf16[2,128,2,512]{3,1,2,0:T(8,128)(2,1)}, bf16[2,128,2,512]{3,1,2,0:T(8,128)(2,1)S(1)}, u32[]{:S(2)}) copy-start(bf16[2,128,2,512]{3,1,2,0:T(8,128)(2,1)S(1)} %fusion.33) | copy-start | bytes 1572868
  218.8 43.7 %copy-start.2 = (bf16[128,1,2048]{2,0,1:T(8,128)(2,1)S(1)}, bf16[128,1,2048]{2,0,1:T(8,128)(2,1)}, u32[]{:S(2)}) copy-start(bf16[128,1,2048]{2,0,1:T(8,128)(2,1)} %param.11) | copy-start | bytes 1572868
  218.8 48.0 %copy-start.4 = (f32[128,1,2048]{2,1,0:T(1,128)S(1)}, f32[128,1,2048]{2,1,0:T(1,128)}, u32[]{:S(2)}) copy-start(f32[128,1,2048]{2,1,0:T(1,128)} %param.21) | copy-start | bytes 3145732
  218.8 152.0 %all-gather.20.cloned.1.call-start = ((), (), s32[]{:S(2)}) async-start(), calls=%async_computation.15 | async-start | bytes 8650752 | tf_op jit(solution)/shard_map/all_gather | solution.py:132
  219.4 180.5 %all-gather.16.cloned.1.call-start = ((), (), s32[]{:S(2)}) async-start(), calls=%async_computation.13 | async-start | bytes 2621440 | tf_op jit(solution)/shard_map/all_gather | solution.py:138
  266.1 242.5 %all-gather.18.cloned.1.call-start = ((), (), s32[]{:S(2)}) async-start(), calls=%async_computation.14 | async-start | bytes 8650752 | tf_op jit(solution)/shard_map/all_gather | solution.py:131
  266.8 271.0 %all-gather.24.cloned.1.call-start = ((), (), s32[]{:S(2)}) async-start(), calls=%async_computation.18 | async-start | bytes 2621440 | tf_op jit(solution)/shard_map/all_gather | solution.py:161
  268.0 378.4 %all-gather.22.cloned.1.call-start = ((), (), s32[]{:S(2)}) async-start(), calls=%async_computation.16 | async-start | bytes 8650752 | tf_op jit(solution)/shard_map/all_gather | solution.py:133
  268.7 449.3 %reduce-scatter.14.cloned.1.call-start = ((), (), s32[]{:S(2)}) async-start(), calls=%async_computation.19 | async-start | bytes 5242880 | tf_op jit(solution)/shard_map/reduce_scatter | solution.py:174
  646.4 13.7 copy-start.19
  660.1 5.0 copy-start.22
  660.1 5.0 copy-start.23
  674.6 75.0 %reduce-scatter.12.cloned.1.call-start = ((), (), s32[]{:S(2)}) async-start(), calls=%async_computation.17 | async-start | bytes 2621440 | tf_op jit(solution)/shard_map/reduce_scatter | solution.py:144
  684.6 98.7 %all-gather.26.cloned.1.call-start = ((), (), s32[]{:S(2)}) async-start(), calls=%async_computation.20 | async-start | bytes 2621440 | tf_op jit(solution)/shard_map/all_gather | solution.py:199
  753.2 89.1 %reduce-scatter.16.cloned.1.call-start = ((), (), s32[]{:S(2)}) async-start(), calls=%async_computation.21 | async-start | bytes 2621440 | tf_op jit(solution)/shard_map/reduce_scatter | solution.py:238
  783.3 3.7 copy-start.1
  794.1 3.8 copy-start.21
  797.8 219.8 %reduce-scatter.20.cloned.1.call-start = ((), (), s32[]{:S(2)}) async-start(), calls=%async_computation.23 | async-start | bytes 2162688 | tf_op jit(solution)/shard_map/reduce_scatter | solution.py:254
  802.1 416.4 %reduce-scatter.24.cloned.1.call-start = ((), (), s32[]{:S(2)}) async-start(), calls=%async_computation.25 | async-start | bytes 8650752 | tf_op jit(solution)/shard_map/reduce_scatter | solution.py:189
  812.5 606.4 %reduce-scatter.22.cloned.1.call-start = ((), (), s32[]{:S(2)}) async-start(), calls=%async_computation.24 | async-start | bytes 8650752 | tf_op jit(solution)/shard_map/reduce_scatter | solution.py:186
  822.6 796.1 %reduce-scatter.26.cloned.1.call-start = ((), (), s32[]{:S(2)}) async-start(), calls=%async_computation.26 | async-start | bytes 8650752 | tf_op jit(solution)/shard_map/reduce_scatter | solution.py:192
  833.0 975.3 %reduce-scatter.18.cloned.1.call-start = ((), (), s32[]{:S(2)}) async-start(), calls=%async_computation.22 | async-start | bytes 4325376 | tf_op jit(solution)/shard_map/reduce_scatter | solution.py:251
  839.1 3.3 copy-start.11
  839.1 3.3 copy-start.16
  839.1 4.7 copy-start.5
  839.1 4.7 copy-start.18
  840.3 178.8 %copy-start.14 = (bf16[2048]{0:T(1024)(128)(2,1)S(1)}, bf16[2048]{0:T(1024)(128)(2,1)}, u32[]{:S(2)}) copy-start(bf16[2048]{0:T(1024)(128)(2,1)} %get-tuple-element.45) | copy-start | bytes 12292
  (10 other events, 14.9 us)
Sparse Core Ops, SparseCore 0:
  11.1 83.3 all-gather.11
  116.1 22.7 all-gather.9
  142.1 71.7 all-gather.13
  219.0 43.5 reduce-scatter.9
  266.0 104.8 all-gather.19
  373.1 26.8 all-gather.15
  403.6 104.8 all-gather.17
  510.9 26.8 all-gather.23
  541.4 104.8 all-gather.21
  674.7 43.2 reduce-scatter.13
  720.4 29.1 reduce-scatter.11
  753.3 29.8 all-gather.25
  797.9 29.2 reduce-scatter.15
  829.4 188.1 reduce-scatter.19
  1020.0 198.5 reduce-scatter.23
  1220.9 197.8 reduce-scatter.21
  1421.2 197.4 reduce-scatter.25
  1621.1 187.2 reduce-scatter.17
where the time goes:
time: 1830 us; the launch traced here: 1820 us
  waiting for transfers between devices  1410 us (77%)
  blocking collectives  198 us (11%)
  matrix products  124 us (7%)
  between operations  37.1 us (2%)
  other arithmetic  29.1 us (2%)
  local copies, waits for them, and re-layouts  22.6 us (1%)
    reduce_scatter x1, waiting for transfers between devices, shards(): lax.psum_scatter(gate_grad.astype(jnp.bfloat16), 'fsdp', scatter_dimensio...  199 us
    reduce_scatter x1, waiting for transfers between devices, shards(): lax.psum_scatter(down_grad.astype(jnp.bfloat16), 'fsdp', scatter_dimensio...  198 us
    unnamed x2, blocking collectives  191 us
    reduce_scatter x1, waiting for transfers between devices, shards(): lax.psum_scatter(joint_grad.astype(jnp.bfloat16), 'fsdp', scatter_dimensi...  188 us
    reduce_scatter x1, waiting for transfers between devices, shards(): lax.psum_scatter(mixing_grad.astype(jnp.bfloat16), 'fsdp', scatter_dimens...  170 us
    all_gather x1, waiting for transfers between devices, shards(): lax.all_gather(down_weight, 'fsdp', axis=1, tiled=True)  109 us
    all_gather x1, waiting for transfers between devices, shards(): lax.all_gather(up_weight, 'fsdp', axis=0, tiled=True)  102 us
    reduce_scatter x1, waiting for transfers between devices, shards(): lax.psum_scatter(upper_grad.astype(jnp.bfloat16), 'fsdp', scatter_dimensi...  102 us
  transfers between devices with their start and end apart: 18, of which 15 were waited for; matrix products, arithmetic and copies ran while one was open for 7% of the time, Pallas kernels for 0%

commit v1 on v0

v1 whole, which is shorter than its diff:
```python
import math

import jax
import jax.numpy as jnp
from jax import lax
from jax.experimental import pallas as pl
from jax.experimental.pallas import tpu as pltpu
from jax.sharding import Mesh
from jax.sharding import PartitionSpec as P

HEADS = 16
KVH = 8
HD = 128
EPSILON = 1e-06
ROPE_BASE = 1000000.0
NEGATIVE = -1e30
MIB = 1024 * 1024

TEAM = ("xh", "xl", "core")
GRID = ("z", "y")

bf16 = jnp.bfloat16
f32 = jnp.float32


def team_swap(value, a, b, c):
    flip = a * 4 + b * 2 + c
    return lax.ppermute(value, TEAM, [(i, i ^ flip) for i in range(8)])


def axis_swap(value, axis, flip):
    return lax.ppermute(value, axis, [(i, i ^ flip) for i in range(4)])


def team_gather(own):
    half = own.shape[0] // 2
    near = team_swap(own, 0, 1, 0)
    next_ = team_swap(own, 1, 1, 0)
    mate = team_swap(own, 0, 0, 1)
    low = team_swap(near[:half], 1, 1, 0)
    high = team_swap(next_[half:], 0, 1, 0)
    near_mate = team_swap(near, 0, 0, 1)
    next_mate = team_swap(next_, 0, 0, 1)
    low_mate = team_swap(low, 0, 0, 1)
    high_mate = team_swap(high, 0, 0, 1)
    return jnp.concatenate(
        [own, mate, near, near_mate, low, high, low_mate, high_mate, next_, next_mate], axis=0
    )


def team_scatter(keep, send):
    got = team_swap(send, 0, 0, 1)
    here = keep[0, 0].astype(f32) + got[0, 0].astype(f32)

    def outgoing(a, b):
        return (keep[a, b].astype(f32) + got[a, b].astype(f32)).astype(bf16)

    near = team_swap(outgoing(0, 1), 0, 1, 0)
    next_ = team_swap(outgoing(1, 1), 1, 1, 0)
    far = team_swap(outgoing(1, 0), 1, 0, 0)
    return here + near.astype(f32) + next_.astype(f32) + far.astype(f32)


def grid_gather(block):
    half = block.shape[1] // 2
    left, right = block[:, :half], block[:, half:]
    left = jnp.concatenate([left] + [axis_swap(left, "y", k) for k in (1, 2, 3)], axis=0)
    right = jnp.concatenate([right] + [axis_swap(right, "z", k) for k in (1, 2, 3)], axis=0)
    return (
        [left] + [axis_swap(left, "z", k) for k in (1, 2, 3)],
        [right] + [axis_swap(right, "y", k) for k in (1, 2, 3)],
    )


def grid_scatter(left, right):
    def one(parts, first, second):
        got = [axis_swap(parts[k], first, k) for k in (1, 2, 3)]
        total = parts[0].astype(f32)
        for item in got:
            total = total + item.astype(f32)
        low = total.astype(bf16)
        got = [axis_swap(low[k], second, k) for k in (1, 2, 3)]
        out = total[0]
        for item in got:
            out = out + item.astype(f32)
        return out

    return jnp.concatenate([one(left, "z", "y"), one(right, "y", "z")], axis=1)


def gather_gains(pair, xh):
    other = team_swap(pair, 1, 0, 0)
    both = jnp.concatenate([jnp.where(xh == 0, pair, other), jnp.where(xh == 0, other, pair)], axis=0)

    def ordered(own, axis):
        me = lax.axis_index(axis)
        got = [own] + [axis_swap(own, axis, k) for k in (1, 2, 3)]
        return jnp.stack([lax.select_n(me ^ k, *got) for k in range(4)])

    whole = ordered(ordered(both, "y"), "z").reshape(32, 128)
    return whole[:, :64].reshape(1, 2048), whole[:, 64:].reshape(1, 2048)


def lane_order(value):
    parts = []
    for z in range(4):
        for y in range(4):
            for xh in range(2):
                start = z * 512 + xh * 256 + y * 64
                parts.append(value[:, start : start + 64])
    return jnp.concatenate(parts, axis=1)


def lane_back(value):
    parts = []
    for z in range(4):
        for xh in range(2):
            for y in range(4):
                start = z * 512 + y * 128 + xh * 64
                parts.append(value[:, start : start + 64])
    return jnp.concatenate(parts, axis=1)


def reorder_kernel(tokens_ref, slope_ref, tokens_out, slope_out, low_out):
    tokens_out[...] = lane_order(tokens_ref[...].astype(f32)).astype(bf16)
    slope = lane_order(slope_ref[...])
    slope_out[...] = slope
    low_out[...] = slope.astype(bf16)


def reorder(tokens, slope):
    shape = tokens.shape
    return pl.pallas_call(
        reorder_kernel,
        out_shape=(
            jax.ShapeDtypeStruct(shape, bf16),
            jax.ShapeDtypeStruct(shape, f32),
            jax.ShapeDtypeStruct(shape, bf16),
        ),
        compiler_params=pltpu.CompilerParams(vmem_limit_bytes=32 * MIB),
    )(tokens, slope)


def tree_tables(lengths, parents, place):
    nseg = lengths.shape[1]
    batch = lengths.shape[0]
    ends = jnp.cumsum(lengths, axis=1)
    starts = ends - lengths
    segment = jnp.sum((place[None, :, None] >= ends[:, None, : nseg - 1]).astype(jnp.int32), axis=2)
    order = jnp.arange(nseg, dtype=jnp.int32)
    rows = [(order == 0).astype(f32)[None, :] * jnp.ones((batch, 1), f32)]
    depth = [jnp.zeros((batch,), jnp.int32)]
    for later in range(1, nseg):
        above = jnp.zeros_like(rows[0])
        reach = jnp.zeros_like(depth[0])
        for earlier in range(later):
            hit = parents[:, later] == earlier
            above = above + hit.astype(f32)[:, None] * rows[earlier]
            reach = reach + jnp.where(hit, depth[earlier] + lengths[:, earlier], 0)
        rows.append(above + (order == later).astype(f32)[None, :])
        depth.append(reach)
    ancestry = jnp.stack(rows, axis=1)
    begin = jnp.stack(depth, axis=1)
    pick = (segment[:, :, None] == order[None, None, :]).astype(f32)
    shift = (begin - starts).astype(f32)
    position = place[None, :].astype(f32) + jnp.sum(pick * shift[:, None, :], axis=2)
    linked = jnp.einsum("bis,bst,bjt->bij", pick, ancestry, pick)
    causal = place[None, :] <= place[:, None]
    return position, ((linked > 0.5) & causal[None]).astype(bf16)


def rotary_tables(position):
    half = HD // 2
    rates = jnp.exp(jnp.arange(half, dtype=f32) * (-2.0 * math.log(ROPE_BASE) / HD))
    angle = position[..., None] * rates
    cosine, sine = jnp.cos(angle), jnp.sin(angle)
    return jnp.concatenate([cosine, cosine], axis=-1), jnp.concatenate([-sine, sine], axis=-1)


def dot(left, right, contract):
    return lax.dot_general(
        left, right, (((contract[0],), (contract[1],)), ((), ())), preferred_element_type=f32
    )


def turn(value, cosine, sine):
    return value * cosine + pltpu.roll(value, HD // 2, 1) * sine


def attend_kernel(
    me_ref, n_ref, l0, l1, l2, l3, r0, r1, r2, r3, cos_ref, sin_ref, mask_ref,
    w_ref, qkv_ref, mixed_ref, keep_ref, send_ref,
):
    z, y = me_ref[0], me_ref[1]

    @pl.when(pl.program_id(0) == 0)
    def _():
        for dz, (left, right) in enumerate(((l0, r0), (l1, r1), (l2, r2), (l3, r3))):
            for dy in range(4):
                first = pl.multiple_of(((z ^ dz) * 4 + (y ^ dy)) * 128, 128)
                w_ref[pl.ds(first, 128), 0:384] = left[dy * 128 : dy * 128 + 128, :]
                second = pl.multiple_of(((z ^ dy) * 4 + (y ^ dz)) * 128, 128)
                w_ref[pl.ds(second, 128), 384:768] = right[dy * 128 : dy * 128 + 128, :]

    joint = dot(n_ref[...], w_ref[:, 0:512], (1, 0))
    cosine, sine = cos_ref[0], sin_ref[0]
    keys = turn(joint[:, 256:384], cosine, sine).astype(bf16)
    values = joint[:, 384:512].astype(bf16)
    qkv_ref[:, 256:384] = keys
    qkv_ref[:, 384:512] = values
    allowed = mask_ref[0].astype(f32) > 0.5
    for head in range(2):
        at = slice(head * HD, head * HD + HD)
        queries = turn(joint[:, at], cosine, sine).astype(bf16)
        qkv_ref[:, at] = queries
        scores = dot(queries, keys, (1, 1)) * (1.0 / math.sqrt(HD))
        scores = jnp.where(allowed, scores, NEGATIVE)
        powers = jnp.exp(scores - jnp.max(scores, axis=1, keepdims=True))
        chance = (powers / jnp.sum(powers, axis=1, keepdims=True)).astype(bf16)
        mixed_ref[:, at] = dot(chance, values, (1, 0)).astype(bf16)
    part = dot(mixed_ref[...], w_ref[:, 512:768], (1, 1)).astype(bf16)
    for b in range(2):
        keep_ref[0, b] = part[b * 256 : b * 256 + 128, :]
        send_ref[0, b] = part[b * 256 + 128 : b * 256 + 256, :]


def attend(me, normed, left, right, cosine, sine, mask):
    whole = lambda shape: pl.BlockSpec(shape, lambda i, me: (0,) * len(shape))
    tree = lambda width: pl.BlockSpec((512, width), lambda i, me: (i, 0))
    table = lambda width: pl.BlockSpec((1, 512, width), lambda i, me: (i, 0, 0))
    quarter = pl.BlockSpec((1, 2, 128, 2048), lambda i, me: (i, 0, 0, 0))
    return pl.pallas_call(
        attend_kernel,
        grid_spec=pltpu.PrefetchScalarGridSpec(
            num_scalar_prefetch=1,
            grid=(2,),
            in_specs=[tree(2048)] + [whole((512, 384))] * 8 + [table(HD), table(HD), table(512)],
            out_specs=[whole((2048, 768)), tree(512), tree(256), quarter, quarter],
        ),
        out_shape=(
            jax.ShapeDtypeStruct((2048, 768), bf16),
            jax.ShapeDtypeStruct((1024, 512), bf16),
            jax.ShapeDtypeStruct((1024, 256), bf16),
            jax.ShapeDtypeStruct((2, 2, 128, 2048), bf16),
            jax.ShapeDtypeStruct((2, 2, 128, 2048), bf16),
        ),
        compiler_params=pltpu.CompilerParams(vmem_limit_bytes=56 * MIB),
        cost_estimate=pl.CostEstimate(
            flops=4 * 1024 * 2048 * 384, bytes_accessed=24 * MIB, transcendentals=1 << 20
        ),
    )(me, normed, *left, *right, cosine, sine, mask)


def attend_back_kernel(
    me_ref, branch_ref, n_ref, w_ref, qkv_ref, mixed_ref, cos_ref, sin_ref, mask_ref,
    left_ref, right_ref, keep_ref, send_ref, js_ref, joint_acc, mixing_acc,
):
    z, y = me_ref[0], me_ref[1]
    step = pl.program_id(0)
    factor = 1.0 / math.sqrt(HD)
    mixed_slope = dot(branch_ref[...], w_ref[:, 512:768], (1, 0)).astype(bf16)
    cosine, sine = cos_ref[0], -sin_ref[0]
    allowed = mask_ref[0].astype(f32) > 0.5
    keys = qkv_ref[:, 256:384]
    values = qkv_ref[:, 384:512]
    key_slope = jnp.zeros((512, HD), f32)
    value_slope = jnp.zeros((512, HD), f32)
    for head in range(2):
        at = slice(head * HD, head * HD + HD)
        queries = qkv_ref[:, at]
        scores = jnp.where(allowed, dot(queries, keys, (1, 1)) * factor, NEGATIVE)
        powers = jnp.exp(scores - jnp.max(scores, axis=1, keepdims=True))
        chance = powers / jnp.sum(powers, axis=1, keepdims=True)
        slope = mixed_slope[:, at]
        value_slope += dot(chance.astype(bf16), slope, (0, 0))
        chance_slope = dot(slope, values, (1, 1))
        balance = jnp.sum(chance * chance_slope, axis=1, keepdims=True)
        score_slope = (chance * (chance_slope - balance)).astype(bf16)
        query_slope = dot(score_slope, keys, (1, 0)) * factor
        js_ref[:, at] = turn(query_slope, cosine, sine).astype(bf16)
        key_slope += dot(score_slope, queries, (0, 0)) * factor
    js_ref[:, 256:384] = turn(key_slope, cosine, sine).astype(bf16)
    js_ref[:, 384:512] = value_slope.astype(bf16)
    joint_slope = js_ref[...]
    joint_part = dot(n_ref[...], joint_slope, (0, 0))
    mixing_part = dot(branch_ref[...], mixed_ref[...], (0, 0))

    @pl.when(step == 0)
    def _():
        joint_acc[...] = joint_part
        mixing_acc[...] = mixing_part

    @pl.when(step == 1)
    def _():
        joint_acc[...] += joint_part
        mixing_acc[...] += mixing_part
        for k in range(4):
            for j in range(4):
                first = pl.multiple_of(((z ^ k) * 4 + (y ^ j)) * 128, 128)
                left_ref[k, j] = joint_acc[pl.ds(first, 128), 0:384].astype(bf16)
                second = pl.multiple_of(((z ^ j) * 4 + (y ^ k)) * 128, 128)
                right_ref[k, j, :, 0:128] = joint_acc[pl.ds(second, 128), 384:512].astype(bf16)
                right_ref[k, j, :, 128:384] = mixing_acc[pl.ds(second, 128), :].astype(bf16)

    part = dot(joint_slope, w_ref[:, 0:512], (1, 1)).astype(bf16)
    for b in range(2):
        keep_ref[0, b] = part[b * 256 : b * 256 + 128, :]
        send_ref[0, b] = part[b * 256 + 128 : b * 256 + 256, :]


def attend_back(me, branch, normed, weights, qkv, mixed, cosine, sine, mask):
    whole = lambda shape: pl.BlockSpec(shape, lambda i, me: (0,) * len(shape))
    tree = lambda width: pl.BlockSpec((512, width), lambda i, me: (i, 0))
    table = lambda width: pl.BlockSpec((1, 512, width), lambda i, me: (i, 0, 0))
    quarter = pl.BlockSpec((1, 2, 128, 2048), lambda i, me: (i, 0, 0, 0))
    return pl.pallas_call(
        attend_back_kernel,
        grid_spec=pltpu.PrefetchScalarGridSpec(
            num_scalar_prefetch=1,
            grid=(2,),
            in_specs=[
                tree(2048), tree(2048), whole((2048, 768)), tree(512), tree(256),
                table(HD), table(HD), table(512),
            ],
            out_specs=[whole((4, 4, 128, 384)), whole((4, 4, 128, 384)), quarter, quarter],
            scratch_shapes=[
                pltpu.VMEM((512, 512), bf16),
                pltpu.VMEM((2048, 512), f32),
                pltpu.VMEM((2048, 256), f32),
            ],
        ),
        out_shape=(
            jax.ShapeDtypeStruct((4, 4, 128, 384), bf16),
            jax.ShapeDtypeStruct((4, 4, 128, 384), bf16),
            jax.ShapeDtypeStruct((2, 2, 128, 2048), bf16),
            jax.ShapeDtypeStruct((2, 2, 128, 2048), bf16),
        ),
        compiler_params=pltpu.CompilerParams(vmem_limit_bytes=56 * MIB),
        cost_estimate=pl.CostEstimate(
            flops=6 * 1024 * 2048 * 512, bytes_accessed=24 * MIB, transcendentals=1 << 20
        ),
    )(me, branch, normed, weights, qkv, mixed, cosine, sine, mask)


def hidden_slope_kernel(x_ref, w_ref, o_ref):
    o_ref[...] = dot(x_ref[...], w_ref[...], (1, 0))


def hidden_slopes(feed, weights):
    return pl.pallas_call(
        hidden_slope_kernel,
        grid=(4,),
        in_specs=[
            pl.BlockSpec((1024, 2048), lambda j: (0, 0)),
            pl.BlockSpec((2048, 256), lambda j: (0, j + 8)),
        ],
        out_specs=pl.BlockSpec((1024, 256), lambda j: (0, j)),
        out_shape=jax.ShapeDtypeStruct((1024, 1024), f32),
        compiler_params=pltpu.CompilerParams(vmem_limit_bytes=48 * MIB),
        cost_estimate=pl.CostEstimate(
            flops=2 * 1024 * 2048 * 1024, bytes_accessed=12 * MIB, transcendentals=0
        ),
    )(feed, weights)


def feed_kernel(n_ref, gate_ref, up_ref, slope_ref, out_ref):
    gate = dot(n_ref[...], gate_ref[...], (1, 0))
    upper = dot(n_ref[...], up_ref[...], (1, 0))
    slope = slope_ref[...]
    sigma = jax.nn.sigmoid(gate)
    active = gate * sigma
    out_ref[0] = (slope * upper * sigma * (1.0 + gate * (1.0 - sigma))).astype(bf16)
    out_ref[1] = (slope * active).astype(bf16)
    out_ref[2] = (active * upper).astype(bf16)


def feed_forward(normed, weights, slopes):
    return pl.pallas_call(
        feed_kernel,
        grid=(4,),
        in_specs=[
            pl.BlockSpec((1024, 2048), lambda j: (0, 0)),
            pl.BlockSpec((2048, 256), lambda j: (0, j)),
            pl.BlockSpec((2048, 256), lambda j: (0, j + 4)),
            pl.BlockSpec((1024, 256), lambda j: (0, j)),
        ],
        out_specs=pl.BlockSpec((3, 1024, 256), lambda j: (0, 0, j)),
        out_shape=jax.ShapeDtypeStruct((3, 1024, 1024), bf16),
        compiler_params=pltpu.CompilerParams(vmem_limit_bytes=48 * MIB),
        cost_estimate=pl.CostEstimate(
            flops=4 * 1024 * 2048 * 1024, bytes_accessed=22 * MIB, transcendentals=1 << 20
        ),
    )(normed, weights, weights, slopes)


def feed_grad_kernel(n_ref, f_ref, s_ref, out_ref, turned):
    step = pl.program_id(0)

    @pl.when(step == 0)
    def _():
        turned[...] = n_ref[...].T

    @pl.when(step == 8)
    def _():
        turned[...] = f_ref[...].T

    out_ref[...] = dot(turned[...], s_ref[0], (1, 0)).astype(bf16)


def feed_grads(normed, feed, slopes):
    return pl.pallas_call(
        feed_grad_kernel,
        grid=(12,),
        in_specs=[
            pl.BlockSpec((1024, 2048), lambda j: (0, 0)),
            pl.BlockSpec((1024, 2048), lambda j: (0, 0)),
            pl.BlockSpec((1, 1024, 256), lambda j: (j // 4, 0, j % 4)),
        ],
        out_specs=pl.BlockSpec((2048, 256), lambda j: (0, j)),
        out_shape=jax.ShapeDtypeStruct((2048, 3072), bf16),
        scratch_shapes=[pltpu.VMEM((2048, 1024), bf16)],
        compiler_params=pltpu.CompilerParams(vmem_limit_bytes=48 * MIB),
        cost_estimate=pl.CostEstimate(
            flops=6 * 1024 * 2048 * 1024, bytes_accessed=26 * MIB, transcendentals=0
        ),
    )(normed, feed, slopes)


def split_rows(part, keep_ref, send_ref):
    for a in range(2):
        for b in range(2):
            first = a * 512 + b * 256
            keep_ref[a, b] = part[first : first + 128, :]
            send_ref[a, b] = part[first + 128 : first + 256, :]


def normed_slope_kernel(g_ref, u_ref, wg_ref, wu_ref, keep_ref, send_ref):
    part = dot(g_ref[0], wg_ref[...], (1, 1)) + dot(u_ref[0], wu_ref[...], (1, 1))
    split_rows(part.astype(bf16), keep_ref, send_ref)


def normed_slopes(slopes, weights):
    half = jax.ShapeDtypeStruct((2, 2, 128, 2048), bf16)
    return pl.pallas_call(
        normed_slope_kernel,
        grid=(8,),
        in_specs=[
            pl.BlockSpec((1, 1024, 1024), lambda j: (0, 0, 0)),
            pl.BlockSpec((1, 1024, 1024), lambda j: (1, 0, 0)),
            pl.BlockSpec((256, 1024), lambda j: (j, 0)),
            pl.BlockSpec((256, 1024), lambda j: (j, 1)),
        ],
        out_specs=[pl.BlockSpec((2, 2, 128, 256), lambda j: (0, 0, 0, j))] * 2,
        out_shape=(half, half),
        compiler_params=pltpu.CompilerParams(vmem_limit_bytes=48 * MIB),
        cost_estimate=pl.CostEstimate(
            flops=4 * 1024 * 2048 * 1024, bytes_accessed=16 * MIB, transcendentals=0
        ),
    )(slopes, slopes, weights, weights)


def down_kernel(h_ref, w_ref, keep_ref, send_ref):
    split_rows(dot(h_ref[0], w_ref[...], (1, 1)).astype(bf16), keep_ref, send_ref)


def down(slopes, weights):
    half = jax.ShapeDtypeStruct((2, 2, 128, 2048), bf16)
    return pl.pallas_call(
        down_kernel,
        grid=(8,),
        in_specs=[
            pl.BlockSpec((1, 1024, 1024), lambda j: (2, 0, 0)),
            pl.BlockSpec((256, 1024), lambda j: (j, 2)),
        ],
        out_specs=[pl.BlockSpec((2, 2, 128, 256), lambda j: (0, 0, 0, j))] * 2,
        out_shape=(half, half),
        compiler_params=pltpu.CompilerParams(vmem_limit_bytes=48 * MIB),
        cost_estimate=pl.CostEstimate(
            flops=2 * 1024 * 2048 * 1024, bytes_accessed=10 * MIB, transcendentals=0
        ),
    )(slopes, weights)


def norm_back(slope, incoming, scale, gain):
    weighted = slope * gain
    cubed = scale * scale * scale
    return scale * weighted - incoming * cubed * jnp.mean(weighted * incoming, axis=1, keepdims=True)


def shards(
    tokens, attend_gain, joint_weight, mixing_weight, feed_gain, gate_weight, up_weight,
    down_weight, lengths, parents, cotangent,
):
    z, y = lax.axis_index("z"), lax.axis_index("y")
    xh, xl, core = lax.axis_index("xh"), lax.axis_index("xl"), lax.axis_index("core")
    me = jnp.stack([z, y]).astype(jnp.int32)

    def both_rows(own, other):
        return jnp.concatenate(
            [jnp.where(xh == 0, own, other), jnp.where(xh == 0, other, own)], axis=0
        )

    def halves(value):
        half = value.shape[1] // 2
        return value[:, :half], value[:, half:]

    def trade(parts):
        first = jnp.concatenate([halves(part)[0] for part in parts], axis=1)
        second = jnp.concatenate([halves(part)[1] for part in parts], axis=1)
        own = jnp.where(xh == 0, first, second)
        other = team_swap(jnp.where(xh == 0, second, first), 1, 0, 0)
        return both_rows(own, other)

    attend_rows = trade([joint_weight, mixing_weight.T])
    left, right = grid_gather(attend_rows)
    feed_rows = trade([gate_weight, up_weight, down_weight.T])
    feed_weights = lax.all_gather(feed_rows, GRID, axis=0, tiled=True)
    gain_one, gain_two = gather_gains(jnp.concatenate([attend_gain, feed_gain])[None], xh)
    gain_one, gain_two = gain_one.astype(f32), gain_two.astype(f32)

    own_tokens, cotangent_own, feed_own = reorder(tokens[:, 0], cotangent[:, 0])
    all_tokens = team_gather(own_tokens)
    trees = jnp.concatenate([lengths, parents], axis=0)
    trees = jnp.stack([trees, team_swap(trees, 1, 0, 0)])
    chunk = jnp.arange(4, dtype=jnp.int32)
    place = ((xl ^ (chunk // 2)) * 2 + (core ^ (chunk % 2))) * 128
    place = (place[:, None] + jnp.arange(128, dtype=jnp.int32)[None]).reshape(512)
    position, mask = tree_tables(trees[:, 0], trees[:, 1], place)
    cosine, sine = rotary_tables(position)

    wide = all_tokens.astype(f32)
    wide_scale = lax.rsqrt(jnp.mean(wide * wide, axis=1, keepdims=True) + EPSILON)
    normed_one = (wide * wide_scale * gain_one).astype(bf16)

    attend_weights, qkv, mixed, keep, send = attend(
        me, normed_one, left, right, cosine, sine, mask
    )
    incoming = own_tokens.astype(f32)
    middle = incoming + team_scatter(keep, send)
    scale_two = lax.rsqrt(jnp.mean(middle * middle, axis=1, keepdims=True) + EPSILON)
    normed_two = team_gather((middle * scale_two * gain_two).astype(bf16))

    feed_all = team_gather(feed_own)
    slopes = hidden_slopes(feed_all, feed_weights)
    slopes = feed_forward(normed_two, feed_weights, slopes)
    feed_grad = feed_grads(normed_two, feed_all, slopes)
    feed_sum = lax.psum_scatter(feed_grad, GRID, scatter_dimension=0, tiled=True)

    middle_slope = cotangent_own + norm_back(
        team_scatter(*normed_slopes(slopes, feed_weights)), middle, scale_two, gain_two
    )
    branch = team_gather(middle_slope.astype(bf16))
    left, right, keep, send = attend_back(
        me, branch, normed_one, attend_weights, qkv, mixed, cosine, sine, mask
    )
    attend_sum = grid_scatter(left, right).astype(bf16)
    scale_one = lax.rsqrt(jnp.mean(incoming * incoming, axis=1, keepdims=True) + EPSILON)
    input_gradient = middle_slope + norm_back(
        team_scatter(keep, send), incoming, scale_one, gain_one
    )
    layer_output = middle + team_scatter(*down(slopes, feed_weights))

    def home(total, widths):
        rows = total.shape[0] // 2
        own = jnp.where(xh == 0, total[:rows], total[rows:])
        other = team_swap(jnp.where(xh == 0, total[rows:], total[:rows]), 1, 0, 0)
        first = jnp.where(xh == 0, own, other).astype(f32)
        second = jnp.where(xh == 0, other, own).astype(f32)
        out, at = [], 0
        for width in widths:
            out.append(
                jnp.concatenate([first[:, at : at + width], second[:, at : at + width]], axis=1)
            )
            at += width
        return out

    gate_grad, up_grad, down_grad = home(feed_sum, (1024, 1024, 1024))
    joint_grad, mixing_grad = home(attend_sum, (512, 256))

    attend_part = jnp.sum(joint_weight.astype(f32) * joint_grad, axis=1)
    feed_part = jnp.sum(
        gate_weight.astype(f32) * gate_grad + up_weight.astype(f32) * up_grad, axis=1
    )
    attend_total, feed_total = lax.psum((attend_part, feed_part), ("xl", "core"))
    return (
        lane_back(layer_output)[:, None],
        lane_back(input_gradient)[:, None],
        attend_total / attend_gain.astype(f32),
        joint_grad,
        mixing_grad.T,
        feed_total / feed_gain.astype(f32),
        gate_grad,
        up_grad,
        down_grad.T,
    )


def solution(mesh):
    fine = Mesh(mesh.devices.reshape(4, 2, 4, 2, 2), ("z", "xh", "y", "xl", "core"))
    fsdp = ("z", "xh", "y")
    tensor = ("xl", "core")
    in_specs = (
        P(tensor, fsdp, None),
        P(fsdp),
        P(fsdp, tensor),
        P(tensor, fsdp),
        P(fsdp),
        P(fsdp, tensor),
        P(fsdp, tensor),
        P(tensor, fsdp),
        P(fsdp, None),
        P(fsdp, None),
        P(tensor, fsdp, None),
    )
    out_specs = (
        P(tensor, fsdp, None),
        P(tensor, fsdp, None),
        P(fsdp),
        P(fsdp, tensor),
        P(tensor, fsdp),
        P(fsdp),
        P(fsdp, tensor),
        P(fsdp, tensor),
        P(tensor, fsdp),
    )
    return jax.shard_map(shards, mesh=fine, in_specs=in_specs, out_specs=out_specs, check_vma=False)
```

time: 1830 us -> 538 us (0.29)
  waiting for transfers between devices: 1410 us -> 218 us
  blocking collectives: 198 us -> 5.67 us
  matrix products: 124 us -> 2.71 us
  Pallas kernels: 0 us -> 102 us
  starting transfers between devices: 1.58 us -> 97.6 us
  local copies, waits for them, and re-layouts: 22.6 us -> 45.9 us
  between operations: 37.1 us -> 15.2 us
    reduce_scatter x9 -> x1, waiting for transfers between devices: 962 us -> 0.02 us  [shards(): lax.psum_scatter(feed_grad, GRID, scatter_dimension=0, tiled=True)]
    all_gather x9 -> x1, waiting for transfers between devices: 440 us -> 0.01 us  [shards(): feed_weights = lax.all_gather(feed_rows, GRID, axis=0, tiled=True)]
    ppermute x0 -> x88, waiting for transfers between devices: none -> 218 us  [the longest x58 155 us: team_swap(): return lax.ppermute(value, TEAM, [(i, i ^ flip) for i in range(8)])]
    unnamed x2 -> x0, blocking collectives: 191 us -> none
    dot_general x22 -> x1, matrix products: 124 us -> 2.71 us  [tree_tables(): linked = jnp.einsum('bis,bst,bjt->bij', pick, ancestry, pick)]
    pallas_call x0 -> x8, Pallas kernels: none -> 102 us  [the longest x1 23 us: attend_back(): pl.pallas_call(attend_back_kernel, grid_spec=pltpu.PrefetchScalarGridSpec...]
    ppermute x0 -> x88, starting transfers between devices: none -> 97.5 us  [the longest x58 53 us: team_swap(): return lax.ppermute(value, TEAM, [(i, i ^ flip) for i in range(8)])]
  transfers between devices with their start and end apart: 18 -> 90, of which waited for: 15 -> 41; matrix products, arithmetic and copies ran while one was open for 7% -> 14% of each run, Pallas kernels for 0% -> 11%
where the time goes in v1:
time: 538 us; the launch traced here: 527 us
  waiting for transfers between devices  218 us (41%)
  Pallas kernels  102 us (19%)
  starting transfers between devices  97.6 us (18%)
  local copies, waits for them, and re-layouts  45.9 us (9%)
  other arithmetic  39.9 us (7%)
  between operations  15.2 us (3%)
  blocking collectives  5.67 us (1%)
    ppermute x58, waiting for transfers between devices, team_swap(): return lax.ppermute(value, TEAM, [(i, i ^ flip) for i in range(8)])  155 us
    ppermute x30, waiting for transfers between devices, axis_swap(): return lax.ppermute(value, axis, [(i, i ^ flip) for i in range(4)])  62.8 us
    ppermute x58, starting transfers between devices, team_swap(): return lax.ppermute(value, TEAM, [(i, i ^ flip) for i in range(8)])  53 us
    ppermute x30, starting transfers between devices, axis_swap(): return lax.ppermute(value, axis, [(i, i ^ flip) for i in range(4)])  44.6 us
    unnamed x99, local copies, waits for them, and re-layouts  29.8 us
    pallas_call x1, Pallas kernels, attend_back(): pl.pallas_call(attend_back_kernel, grid_spec=pltpu.PrefetchScalarGridSpec...  23 us
    pallas_call x1, Pallas kernels, feed_grads(): pl.pallas_call(feed_grad_kernel, grid=(12,), in_specs=[pl.BlockSpec((1024...  22.1 us
    pallas_call x1, Pallas kernels, feed_forward(): pl.pallas_call(feed_kernel, grid=(4,), in_specs=[pl.BlockSpec((1024, 2048...  13.5 us
  transfers between devices with their start and end apart: 90, of which 41 were waited for; matrix products, arithmetic and copies ran while one was open for 14% of the time, Pallas kernels for 11%

profile of v1, /device:TPU:0, one launch (start us, length us, event | category | flops | bytes accessed | tf_op | source)
XLA Modules:
  0.0 527.3 jit_solution(18323648426333501441)
XLA Ops:
  12.8 9.1 %collective-permute-done.43 = bf16[64,3072]{1,0:T(8,128)(2,1)S(1)} collective-permute-done((bf16[64,3072]{1,0:T(8,128)(2,1)S(1)}, bf16[64,3072]{1,0:T(8,128)(2,1)S(1)}, u32[]{:S(2)}, u32[]{:S(2)}) %collective-permute-start.43) | collective-permute-done | bytes 393248 | tf_op jit(solution)/shard_map/ppermute | solution.py:28
  34.3 7.8 %collective-permute-done.29 = s32[2,7]{1,0:T(2,128)S(1)} collective-permute-done((s32[2,7]{1,0:T(2,128)S(1)}, s32[2,7]{1,0:T(2,128)S(1)}, u32[]{:S(2)}, u32[]{:S(2)}) %collective-permute-start.29) | collective-permute-done | bytes 88 | tf_op jit(solution)/shard_map/ppermute | solution.py:28
  58.2 3.6 collective-permute-start.14
  66.6 4.6 collective-permute-done.16
  72.6 7.4 %collective-permute-done.19 = bf16[128,384]{1,0:T(8,128)(2,1)S(1)} collective-permute-done((bf16[128,384]{1,0:T(8,128)(2,1)S(1)}, bf16[128,384]{1,0:T(8,128)(2,1)S(1)}, u32[]{:S(2)}, u32[]{:S(2)}) %collective-permute-start.19) | collective-permute-done | bytes 98336 | tf_op jit(solution)/shard_map/ppermute | solution.py:32
  96.3 4.4 collective-permute-done.23
  139.2 8.1 %collective-permute-done.28.r3 = bf16[512,384]{1,0:T(8,128)(2,1)S(1)} collective-permute-done((bf16[512,384]{1,0:T(8,128)(2,1)S(1)}, bf16[512,384]{1,0:T(8,128)(2,1)S(1)}, u32[]{:S(2)}, u32[]{:S(2)}) %collective-permute-start.28) | collective-permute-done | bytes 393248 | tf_op jit(solution)/shard_map/ppermute | solution.py:32
  148.1 12.8 %shard_map.179 = (bf16[2048,768]{1,0:T(8,128)(2,1)}, bf16[1024,512]{1,0:T(8,128)(2,1)}, bf16[1024,256]{1,0:T(8,128)(2,1)}, bf16[2,2,128,2048]{3,2,1,0:T(8,128)(2,1)}, bf16[2,2,128,2048]{3,2,1,0:T(8,128)(2,1)}) custom-call(s32[2]{0:T(128)} %pad_add_fusion.2.me_ref, bf16[1024,2048]{1,0:T(8,128)(2,1)} %fusion.2.n_ref, bf16[512,384]{1,0:T(8,128)(2,1)} %copy-done.13, ...), custom_call_target="tpu_custom_call" | custom-call | flops 3221225472 | bytes 25165824 | tf_op jit(solution)/shard_map/pallas_call | solution.py:232
  163.5 11.9 %collective-permute-done.45 = bf16[128,2048]{1,0:T(8,128)(2,1)S(1)} collective-permute-done((bf16[128,2048]{1,0:T(8,128)(2,1)S(1)}, bf16[128,2048]{1,0:T(8,128)(2,1)S(1)}, u32[]{:S(2)}, u32[]{:S(2)}) %collective-permute-start.45) | collective-permute-done | bytes 524320 | tf_op jit(solution)/shard_map/ppermute | solution.py:28
  190.0 8.9 %collective-permute-done.33 = bf16[128,2048]{1,0:T(8,128)(2,1)S(1)} collective-permute-done((bf16[128,2048]{1,0:T(8,128)(2,1)S(1)}, bf16[128,2048]{1,0:T(8,128)(2,1)S(1)}, u32[]{:S(2)}, u32[]{:S(2)}) %collective-permute-start.33) | collective-permute-done | bytes 524320 | tf_op jit(solution)/shard_map/ppermute | solution.py:28
  198.9 10.8 %collective-permute-done.32 = bf16[128,2048]{1,0:T(8,128)(2,1)S(1)} collective-permute-done((bf16[128,2048]{1,0:T(8,128)(2,1)S(1)}, bf16[128,2048]{1,0:T(8,128)(2,1)S(1)}, u32[]{:S(2)}, u32[]{:S(2)}) %collective-permute-start.32) | collective-permute-done | bytes 524320 | tf_op jit(solution)/shard_map/ppermute | solution.py:28
  217.2 8.2 %collective-permute-done.35 = bf16[128,2048]{1,0:T(8,128)(2,1)S(1)} collective-permute-done((bf16[128,2048]{1,0:T(8,128)(2,1)S(1)}, bf16[128,2048]{1,0:T(8,128)(2,1)S(1)}, u32[]{:S(2)}, u32[]{:S(2)}) %collective-permute-start.35) | collective-permute-done | bytes 524320 | tf_op jit(solution)/shard_map/ppermute | solution.py:28
  229.3 7.0 %collective-permute-done.37 = bf16[64,2048]{1,0:T(8,128)(2,1)S(1)} collective-permute-done((bf16[64,2048]{1,0:T(8,128)(2,1)S(1)}, bf16[64,2048]{1,0:T(8,128)(2,1)S(1)}, u32[]{:S(2)}, u32[]{:S(2)}) %collective-permute-start.37) | collective-permute-done | bytes 262176 | tf_op jit(solution)/shard_map/ppermute | solution.py:28
  240.5 8.0 %shard_map.180.slope_ref = f32[1024,1024]{1,0:T(8,128)S(1)} custom-call(bf16[1024,2048]{1,0:T(8,128)(2,1)} %constant_dynamic-update-slice_fusion.27.x_ref.f_ref, bf16[2048,3072]{1,0:T(8,128)(2,1)} %all-gather.2.cloned.1.call-done.w_ref.gate_ref.up_ref.wg_ref.wu_ref), custom_call_target="tpu_custom_call" | custom-call | flops 4294967296 | bytes 12582912 | tf_op jit(solution)/shard_map/pallas_call | solution.py:350
  250.5 13.5 %shard_map.181.h_ref.g_ref.u_ref.s_ref = bf16[3,1024,1024]{2,1,0:T(8,128)(2,1)} custom-call(bf16[1024,2048]{1,0:T(8,128)(2,1)S(1)} %copy-done.2, bf16[2048,3072]{1,0:T(8,128)(2,1)} %all-gather.2.cloned.1.call-done.w_ref.gate_ref.up_ref.wg_ref.wu_ref, bf16[2048,3072]{1,0:T(8,128)(2,1)} %all-gather.2.cloned.1.call-done.w_ref.gate_ref.up_ref.wg_ref.wu_ref, ...), custom_call_target="tpu_custom_call" | custom-call | flops 8589934592 | bytes 23068672 | tf_op jit(solution)/shard_map/pallas_call | solution.py:378
  264.1 22.1 %shard_map.185 = bf16[2048,3072]{1,0:T(8,128)(2,1)} custom-call(bf16[1024,2048]{1,0:T(8,128)(2,1)S(1)} %copy-done.2, bf16[1024,2048]{1,0:T(8,128)(2,1)} %constant_dynamic-update-slice_fusion.27.x_ref.f_ref, bf16[3,1024,1024]{2,1,0:T(8,128)(2,1)} %shard_map.181.h_ref.g_ref.u_ref.s_ref), custom_call_target="tpu_custom_call" | custom-call | flops 12884901888 | bytes 27262976 | tf_op jit(solution)/shard_map/pallas_call | solution.py:411
  286.2 13.4 %shard_map.183 = (bf16[2,2,128,2048]{3,2,1,0:T(8,128)(2,1)S(1)}, bf16[2,2,128,2048]{3,2,1,0:T(8,128)(2,1)S(1)}) custom-call(bf16[3,1024,1024]{2,1,0:T(8,128)(2,1)} %shard_map.181.h_ref.g_ref.u_ref.s_ref, bf16[3,1024,1024]{2,1,0:T(8,128)(2,1)} %shard_map.181.h_ref.g_ref.u_ref.s_ref, ...), custom_call_target="tpu_custom_call" | custom-call | flops 8589934592 | bytes 16777216 | tf_op jit(solution)/shard_map/pallas_call | solution.py:444
  299.9 9.1 %shard_map.182 = (bf16[2,2,128,2048]{3,2,1,0:T(8,128)(2,1)S(1)}, bf16[2,2,128,2048]{3,2,1,0:T(8,128)(2,1)S(1)}) custom-call(bf16[3,1024,1024]{2,1,0:T(8,128)(2,1)} %shard_map.181.h_ref.g_ref.u_ref.s_ref, bf16[2048,3072]{1,0:T(8,128)(2,1)} %all-gather.2.cloned.1.call-done.w_ref.gate_ref.up_ref.wg_ref.wu_ref), custom_call_target="tpu_custom_call" | custom-call | flops 4294967296 | bytes 10485760 | tf_op jit(solution)/shard_map/pallas_call | solution.py:468
  318.9 7.6 %collective-permute-done.60 = bf16[128,2048]{1,0:T(8,128)(2,1)S(1)} collective-permute-done((bf16[128,2048]{1,0:T(8,128)(2,1)S(1)}, bf16[128,2048]{1,0:T(8,128)(2,1)S(1)}, u32[]{:S(2)}, u32[]{:S(2)}) %collective-permute-start.60) | collective-permute-done | bytes 524320 | tf_op jit(solution)/shard_map/ppermute | solution.py:28
  326.7 11.0 %collective-permute-done.59 = bf16[128,2048]{1,0:T(8,128)(2,1)S(1)} collective-permute-done((bf16[128,2048]{1,0:T(8,128)(2,1)S(1)}, bf16[128,2048]{1,0:T(8,128)(2,1)S(1)}, u32[]{:S(2)}, u32[]{:S(2)}) %collective-permute-start.59) | collective-permute-done | bytes 524320 | tf_op jit(solution)/shard_map/ppermute | solution.py:28
  337.8 11.2 %collective-permute-done.56 = bf16[128,2048]{1,0:T(8,128)(2,1)S(1)} collective-permute-done((bf16[128,2048]{1,0:T(8,128)(2,1)S(1)}, bf16[128,2048]{1,0:T(8,128)(2,1)S(1)}, u32[]{:S(2)}, u32[]{:S(2)}) %collective-permute-start.56) | collective-permute-done | bytes 524320 | tf_op jit(solution)/shard_map/ppermute | solution.py:28
  349.0 10.4 %collective-permute-done.55 = bf16[128,2048]{1,0:T(8,128)(2,1)S(1)} collective-permute-done((bf16[128,2048]{1,0:T(8,128)(2,1)S(1)}, bf16[128,2048]{1,0:T(8,128)(2,1)S(1)}, u32[]{:S(2)}, u32[]{:S(2)}) %collective-permute-start.55) | collective-permute-done | bytes 524320 | tf_op jit(solution)/shard_map/ppermute | solution.py:28
  365.6 10.3 %collective-permute-done.62 = bf16[128,2048]{1,0:T(8,128)(2,1)S(1)} collective-permute-done((bf16[128,2048]{1,0:T(8,128)(2,1)S(1)}, bf16[128,2048]{1,0:T(8,128)(2,1)S(1)}, u32[]{:S(2)}, u32[]{:S(2)}) %collective-permute-start.62) | collective-permute-done | bytes 524320 | tf_op jit(solution)/shard_map/ppermute | solution.py:28
  379.5 7.1 %collective-permute-done.64 = bf16[64,2048]{1,0:T(8,128)(2,1)S(1)} collective-permute-done((bf16[64,2048]{1,0:T(8,128)(2,1)S(1)}, bf16[64,2048]{1,0:T(8,128)(2,1)S(1)}, u32[]{:S(2)}, u32[]{:S(2)}) %collective-permute-start.64) | collective-permute-done | bytes 262176 | tf_op jit(solution)/shard_map/ppermute | solution.py:28
  391.3 23.0 %shard_map.184 = (bf16[4,4,128,384]{3,2,1,0:T(8,128)(2,1)}, bf16[4,4,128,384]{3,2,1,0:T(8,128)(2,1)}, bf16[2,2,128,2048]{3,2,1,0:T(8,128)(2,1)}, bf16[2,2,128,2048]{3,2,1,0:T(8,128)(2,1)}) custom-call(s32[2]{0:T(128)} %pad_add_fusion.2.me_ref, bf16[1024,2048]{1,0:T(8,128)(2,1)} %copy-done.18, bf16[1024,2048]{1,0:T(8,128)(2,1)} %fusion.2.n_ref, ...), custom_call_target="tpu_custom_call" | custom-call | flops 6442450944 | bytes 25165824 | tf_op jit(solution)/shard_map/pallas_call | solution.py:316
  428.2 10.0 %collective-permute-done.82 = bf16[4,128,384]{2,1,0:T(8,128)(2,1)} collective-permute-done((bf16[4,128,384]{2,1,0:T(8,128)(2,1)}, bf16[4,128,384]{2,1,0:T(8,128)(2,1)}, u32[]{:S(2)}, u32[]{:S(2)}) %collective-permute-start.82) | collective-permute-done | bytes 393248 | tf_op jit(solution)/shard_map/ppermute | solution.py:32
  446.9 4.9 collective-permute-done.75
  452.7 7.3 %collective-permute-done.74 = bf16[4,128,384]{2,1,0:T(8,128)(2,1)S(1)} collective-permute-done((bf16[4,128,384]{2,1,0:T(8,128)(2,1)S(1)}, bf16[4,128,384]{2,1,0:T(8,128)(2,1)S(1)}, u32[]{:S(2)}, u32[]{:S(2)}) %collective-permute-start.74) | collective-permute-done | bytes 393248 | tf_op jit(solution)/shard_map/ppermute | solution.py:32
  477.9 9.6 %collective-permute-done.73 = bf16[128,2048]{1,0:T(8,128)(2,1)S(1)} collective-permute-done((bf16[128,2048]{1,0:T(8,128)(2,1)S(1)}, bf16[128,2048]{1,0:T(8,128)(2,1)S(1)}, u32[]{:S(2)}, u32[]{:S(2)}) %collective-permute-start.73) | collective-permute-done | bytes 524320 | tf_op jit(solution)/shard_map/ppermute | solution.py:28
  487.5 6.5 %collective-permute-done.72 = bf16[128,2048]{1,0:T(8,128)(2,1)S(1)} collective-permute-done((bf16[128,2048]{1,0:T(8,128)(2,1)S(1)}, bf16[128,2048]{1,0:T(8,128)(2,1)S(1)}, u32[]{:S(2)}, u32[]{:S(2)}) %collective-permute-start.72) | collective-permute-done | bytes 524320 | tf_op jit(solution)/shard_map/ppermute | solution.py:28
  507.0 4.3 collective-permute-done.87
  512.7 5.7 %all-reduce = (f32[64]{0:T(128)S(1)}, f32[64]{0:T(128)S(1)}) all-reduce(f32[64]{0:T(128)S(1)} %copy-done.24, f32[64]{0:T(128)S(1)} %get-tuple-element.102), channel_id=1, replica_groups=mesh['z'=4,'xh'=2,'y'=4,'xl'=2,'core'=2] {'xl','core'}, use_global_device_ids=true, to_apply=%region_9.10 | all-reduce | flops 128 | bytes 1024 | tf_op jit(solution)/shard_map/psum | solution.py:584
  (373 shorter events, 212.4 us)
Async XLA Ops:
  7.2 233.4 %all-gather.2.cloned.1.call-start = ((), (), s32[]{:S(2)}) async-start(), calls=%async_computation.1 | async-start | bytes 13369344 | tf_op jit(solution)/shard_map/all_gather | solution.py:517
  23.1 474.6 %reduce-scatter.2.cloned.1.call-start = ((), (), s32[]{:S(2)}) async-start(), calls=%async_computation.2 | async-start | bytes 13369344 | tf_op jit(solution)/shard_map/reduce_scatter | solution.py:547
  25.2 80.3 %collective-permute-start = (bf16[128,2048]{1,0:T(8,128)(2,1)S(1)}, bf16[128,2048]{1,0:T(8,128)(2,1)}, u32[]{:S(2)}, u32[]{:S(2)}) collective-permute-start(bf16[128,2048]{1,0:T(8,128)(2,1)S(1)} %get-tuple-element.25), channel_id=1, source_target_pairs={{0,1},{1,0},{2,3},{3,2},{16,17},{17,16},{18,19},{19,18},{4,5},{5,4... | collective-permute-start | bytes 1572872 | tf_op jit(solution)/shard_map/ppermute | solution.py:28
  25.3 75.8 %collective-permute-start.1 = (bf16[128,2048]{1,0:T(8,128)(2,1)S(1)}, bf16[128,2048]{1,0:T(8,128)(2,1)}, u32[]{:S(2)}, u32[]{:S(2)}) collective-permute-start(bf16[128,2048]{1,0:T(8,128)(2,1)S(1)} %get-tuple-element.25), channel_id=1, source_target_pairs={{0,2},{1,3},{2,0},{3,1},{16,18},{17,19},{18,16},{19,17},{4,6},{5,7... | collective-permute-start | bytes 1572872 | tf_op jit(solution)/shard_map/ppermute | solution.py:28
  27.2 19.6 %collective-permute-start.9 = (bf16[1,128]{1,0:T(2,128)(2,1)S(1)}, bf16[1,128]{1,0:T(2,128)(2,1)S(1)}, u32[]{:S(2)}, u32[]{:S(2)}) collective-permute-start(bf16[1,128]{1,0:T(2,128)(2,1)S(1)} %maximum_bitcast_fusion.2), channel_id=1, source_target_pairs={{0,16},{1,17},{2,18},{3,19},{16,0},{17,1},{18,2},{19,3},{4,20},{5,... | collective-permute-start | bytes 776 | tf_op jit(solution)/shard_map/ppermute | solution.py:28
  64.6 37.7 %collective-permute-start.4 = (bf16[128,2048]{1,0:T(8,128)(2,1)S(1)}, bf16[128,2048]{1,0:T(8,128)(2,1)S(1)}, u32[]{:S(2)}, u32[]{:S(2)}) collective-permute-start(bf16[128,2048]{1,0:T(8,128)(2,1)S(1)} %get-tuple-element.25), channel_id=1, source_target_pairs={{0,18},{1,19},{2,16},{3,17},{16,2},{17,3},{18,0},{19,1},{4,22},{5,... | collective-permute-start | bytes 1572872 | tf_op jit(solution)/shard_map/ppermute | solution.py:28
  95.4 31.4 %collective-permute-start.20 = (bf16[512,384]{1,0:T(8,128)(2,1)S(1)}, bf16[512,384]{1,0:T(8,128)(2,1)S(1)}, u32[]{:S(2)}, u32[]{:S(2)}) collective-permute-start(bf16[512,384]{1,0:T(8,128)(2,1)S(1)} %pad_maximum_fusion.5.l0), channel_id=1, source_target_pairs={{0,32},{32,0},{64,96},{96,64},{1,33},{33,1},{65,97},{97,65},{2,34}... | collective-permute-start | bytes 1179656 | tf_op jit(solution)/shard_map/ppermute | solution.py:32
  100.6 32.9 %collective-permute-start.21 = (bf16[512,384]{1,0:T(8,128)(2,1)S(1)}, bf16[512,384]{1,0:T(8,128)(2,1)S(1)}, u32[]{:S(2)}, u32[]{:S(2)}) collective-permute-start(bf16[512,384]{1,0:T(8,128)(2,1)S(1)} %pad_maximum_fusion.5.l0), channel_id=1, source_target_pairs={{0,64},{32,96},{64,0},{96,32},{1,65},{33,97},{65,1},{97,33},{2,66}... | collective-permute-start | bytes 1179656 | tf_op jit(solution)/shard_map/ppermute | solution.py:32
  112.5 24.1 %collective-permute-start.22 = (bf16[512,384]{1,0:T(8,128)(2,1)S(1)}, bf16[512,384]{1,0:T(8,128)(2,1)S(1)}, u32[]{:S(2)}, u32[]{:S(2)}) collective-permute-start(bf16[512,384]{1,0:T(8,128)(2,1)S(1)} %pad_maximum_fusion.5.l0), channel_id=1, source_target_pairs={{0,96},{32,64},{64,32},{96,0},{1,97},{33,65},{65,33},{97,1},{2,98}... | collective-permute-start | bytes 1179656 | tf_op jit(solution)/shard_map/ppermute | solution.py:32
  118.8 17.8 %collective-permute-start.26 = (bf16[512,384]{1,0:T(8,128)(2,1)S(1)}, bf16[512,384]{1,0:T(8,128)(2,1)S(1)}, u32[]{:S(2)}, u32[]{:S(2)}) collective-permute-start(bf16[512,384]{1,0:T(8,128)(2,1)S(1)} %pad_maximum_fusion.6.r0), channel_id=1, source_target_pairs={{0,4},{4,0},{8,12},{12,8},{1,5},{5,1},{9,13},{13,9},{2,6},{6,2},{1... | collective-permute-start | bytes 1179656 | tf_op jit(solution)/shard_map/ppermute | solution.py:32
  120.4 18.9 %collective-permute-start.27 = (bf16[512,384]{1,0:T(8,128)(2,1)S(1)}, bf16[512,384]{1,0:T(8,128)(2,1)S(1)}, u32[]{:S(2)}, u32[]{:S(2)}) collective-permute-start(bf16[512,384]{1,0:T(8,128)(2,1)S(1)} %pad_maximum_fusion.6.r0), channel_id=1, source_target_pairs={{0,8},{4,12},{8,0},{12,4},{1,9},{5,13},{9,1},{13,5},{2,10},{6,14},... | collective-permute-start | bytes 1179656 | tf_op jit(solution)/shard_map/ppermute | solution.py:32
  126.9 20.5 %collective-permute-start.28 = (bf16[512,384]{1,0:T(8,128)(2,1)S(1)}, bf16[512,384]{1,0:T(8,128)(2,1)S(1)}, u32[]{:S(2)}, u32[]{:S(2)}) collective-permute-start(bf16[512,384]{1,0:T(8,128)(2,1)S(1)} %pad_maximum_fusion.6.r0), channel_id=1, source_target_pairs={{0,12},{4,8},{8,4},{12,0},{1,13},{5,9},{9,5},{13,1},{2,14},{6,10},... | collective-permute-start | bytes 1179656 | tf_op jit(solution)/shard_map/ppermute | solution.py:32
  160.9 19.6 %collective-permute-start.30 = (bf16[2,2,128,2048]{3,2,1,0:T(8,128)(2,1)}, bf16[2,2,128,2048]{3,2,1,0:T(8,128)(2,1)}, u32[]{:S(2)}, u32[]{:S(2)}) collective-permute-start(bf16[2,2,128,2048]{3,2,1,0:T(8,128)(2,1)} %get-tuple-element.27), channel_id=1, source_target_pairs={{0,1},{1,0},{2,3},{3,2},{16,17},{17,16},{18,19},{19,18},{4,5},{5,4... | collective-permute-start | bytes 6291464 | tf_op jit(solution)/shard_map/ppermute | solution.py:28
  185.0 24.6 %collective-permute-start.32 = (bf16[128,2048]{1,0:T(8,128)(2,1)S(1)}, bf16[128,2048]{1,0:T(8,128)(2,1)S(1)}, u32[]{:S(2)}, u32[]{:S(2)}) collective-permute-start(bf16[128,2048]{1,0:T(8,128)(2,1)S(1)} %get-tuple-element.143), channel_id=1, source_target_pairs={{0,18},{1,19},{2,16},{3,17},{16,2},{17,3},{18,0},{19,1},{4,22},{5,... | collective-permute-start | bytes 1572872 | tf_op jit(solution)/shard_map/ppermute | solution.py:28
  187.2 22.5 %collective-permute-start.31 = (bf16[128,2048]{1,0:T(8,128)(2,1)S(1)}, bf16[128,2048]{1,0:T(8,128)(2,1)S(1)}, u32[]{:S(2)}, u32[]{:S(2)}) collective-permute-start(bf16[128,2048]{1,0:T(8,128)(2,1)S(1)} %get-tuple-element.141), channel_id=1, source_target_pairs={{0,2},{1,3},{2,0},{3,1},{16,18},{17,19},{18,16},{19,17},{4,6},{5,7... | collective-permute-start | bytes 1572872 | tf_op jit(solution)/shard_map/ppermute | solution.py:28
  188.0 37.3 %collective-permute-start.52 = (bf16[128,2048]{1,0:T(8,128)(2,1)S(1)}, bf16[128,2048]{1,0:T(8,128)(2,1)S(1)}, u32[]{:S(2)}, u32[]{:S(2)}) collective-permute-start(bf16[128,2048]{1,0:T(8,128)(2,1)S(1)} %collective-permute-done.48), channel_id=1, source_target_pairs={{0,1},{1,0},{2,3},{3,2},{16,17},{17,16},{18,19},{19,18},{4,5},{5,4... | collective-permute-start | bytes 1572872 | tf_op jit(solution)/shard_map/ppermute | solution.py:28
  188.8 23.8 %collective-permute-start.50 = (bf16[64,2048]{1,0:T(8,128)(2,1)S(1)}, bf16[64,2048]{1,0:T(8,128)(2,1)S(1)}, u32[]{:S(2)}, u32[]{:S(2)}) collective-permute-start(bf16[64,2048]{1,0:T(8,128)(2,1)S(1)} %collective-permute-done.47), channel_id=1, source_target_pairs={{0,1},{1,0},{2,3},{3,2},{16,17},{17,16},{18,19},{19,18},{4,5},{5,4... | collective-permute-start | bytes 786440 | tf_op jit(solution)/shard_map/ppermute | solution.py:28
  312.0 25.7 %collective-permute-start.59 = (bf16[128,2048]{1,0:T(8,128)(2,1)S(1)}, bf16[128,2048]{1,0:T(8,128)(2,1)S(1)}, u32[]{:S(2)}, u32[]{:S(2)}) collective-permute-start(bf16[128,2048]{1,0:T(8,128)(2,1)S(1)} %get-tuple-element.137), channel_id=1, source_target_pairs={{0,18},{1,19},{2,16},{3,17},{16,2},{17,3},{18,0},{19,1},{4,22},{5,... | collective-permute-start | bytes 1572872 | tf_op jit(solution)/shard_map/ppermute | solution.py:28
  313.1 24.7 %collective-permute-start.58 = (bf16[128,2048]{1,0:T(8,128)(2,1)S(1)}, bf16[128,2048]{1,0:T(8,128)(2,1)S(1)}, u32[]{:S(2)}, u32[]{:S(2)}) collective-permute-start(bf16[128,2048]{1,0:T(8,128)(2,1)S(1)} %get-tuple-element.135), channel_id=1, source_target_pairs={{0,2},{1,3},{2,0},{3,1},{16,18},{17,19},{18,16},{19,17},{4,6},{5,7... | collective-permute-start | bytes 1572872 | tf_op jit(solution)/shard_map/ppermute | solution.py:28
  314.6 34.4 %collective-permute-start.56 = (bf16[128,2048]{1,0:T(8,128)(2,1)S(1)}, bf16[128,2048]{1,0:T(8,128)(2,1)S(1)}, u32[]{:S(2)}, u32[]{:S(2)}) collective-permute-start(bf16[128,2048]{1,0:T(8,128)(2,1)S(1)} %get-tuple-element.139), channel_id=1, source_target_pairs={{0,16},{1,17},{2,18},{3,19},{16,0},{17,1},{18,2},{19,3},{4,20},{5,... | collective-permute-start | bytes 1572872 | tf_op jit(solution)/shard_map/ppermute | solution.py:28
  317.8 41.5 %collective-permute-start.55 = (bf16[128,2048]{1,0:T(8,128)(2,1)S(1)}, bf16[128,2048]{1,0:T(8,128)(2,1)S(1)}, u32[]{:S(2)}, u32[]{:S(2)}) collective-permute-start(bf16[128,2048]{1,0:T(8,128)(2,1)S(1)} %get-tuple-element.140), channel_id=1, source_target_pairs={{0,18},{1,19},{2,16},{3,17},{16,2},{17,3},{18,0},{19,1},{4,22},{5,... | collective-permute-start | bytes 1572872 | tf_op jit(solution)/shard_map/ppermute | solution.py:28
  326.5 32.9 %collective-permute-start.54 = (bf16[128,2048]{1,0:T(8,128)(2,1)S(1)}, bf16[128,2048]{1,0:T(8,128)(2,1)S(1)}, u32[]{:S(2)}, u32[]{:S(2)}) collective-permute-start(bf16[128,2048]{1,0:T(8,128)(2,1)S(1)} %get-tuple-element.138), channel_id=1, source_target_pairs={{0,2},{1,3},{2,0},{3,1},{16,18},{17,19},{18,16},{19,17},{4,6},{5,7... | collective-permute-start | bytes 1572872 | tf_op jit(solution)/shard_map/ppermute | solution.py:28
  414.3 54.7 %collective-permute-start.70 = (bf16[2,2,128,2048]{3,2,1,0:T(8,128)(2,1)}, bf16[2,2,128,2048]{3,2,1,0:T(8,128)(2,1)}, u32[]{:S(2)}, u32[]{:S(2)}) collective-permute-start(bf16[2,2,128,2048]{3,2,1,0:T(8,128)(2,1)} %get-tuple-element.38), channel_id=1, source_target_pairs={{0,1},{1,0},{2,3},{3,2},{16,17},{17,16},{18,19},{19,18},{4,5},{5,4... | collective-permute-start | bytes 6291464 | tf_op jit(solution)/shard_map/ppermute | solution.py:28
  416.9 21.3 %collective-permute-start.82 = (bf16[4,128,384]{2,1,0:T(8,128)(2,1)}, bf16[4,128,384]{2,1,0:T(8,128)(2,1)}, u32[]{:S(2)}, u32[]{:S(2)}) collective-permute-start(bf16[4,128,384]{2,1,0:T(8,128)(2,1)} %get-tuple-element.148), channel_id=1, source_target_pairs={{0,12},{4,8},{8,4},{12,0},{1,13},{5,9},{9,5},{13,1},{2,14},{6,10},... | collective-permute-start | bytes 1179656 | tf_op jit(solution)/shard_map/ppermute | solution.py:32
  419.6 21.3 %collective-permute-start.81 = (bf16[4,128,384]{2,1,0:T(8,128)(2,1)}, bf16[4,128,384]{2,1,0:T(8,128)(2,1)}, u32[]{:S(2)}, u32[]{:S(2)}) collective-permute-start(bf16[4,128,384]{2,1,0:T(8,128)(2,1)} %get-tuple-element.149), channel_id=1, source_target_pairs={{0,8},{4,12},{8,0},{12,4},{1,9},{5,13},{9,1},{13,5},{2,10},{6,14},... | collective-permute-start | bytes 1179656 | tf_op jit(solution)/shard_map/ppermute | solution.py:32
  419.6 21.9 %collective-permute-start.80 = (bf16[4,128,384]{2,1,0:T(8,128)(2,1)}, bf16[4,128,384]{2,1,0:T(8,128)(2,1)}, u32[]{:S(2)}, u32[]{:S(2)}) collective-permute-start(bf16[4,128,384]{2,1,0:T(8,128)(2,1)} %get-tuple-element.147), channel_id=1, source_target_pairs={{0,4},{4,0},{8,12},{12,8},{1,5},{5,1},{9,13},{13,9},{2,6},{6,2},{1... | collective-permute-start | bytes 1179656 | tf_op jit(solution)/shard_map/ppermute | solution.py:32
  425.7 18.4 %collective-permute-start.76 = (bf16[4,128,384]{2,1,0:T(8,128)(2,1)S(1)}, bf16[4,128,384]{2,1,0:T(8,128)(2,1)S(1)}, u32[]{:S(2)}, u32[]{:S(2)}) collective-permute-start(bf16[4,128,384]{2,1,0:T(8,128)(2,1)S(1)} %get-tuple-element.145), channel_id=1, source_target_pairs={{0,96},{32,64},{64,32},{96,0},{1,97},{33,65},{65,33},{97,1},{2,98}... | collective-permute-start | bytes 1179656 | tf_op jit(solution)/shard_map/ppermute | solution.py:32
  440.9 19.1 %collective-permute-start.74 = (bf16[4,128,384]{2,1,0:T(8,128)(2,1)S(1)}, bf16[4,128,384]{2,1,0:T(8,128)(2,1)S(1)}, u32[]{:S(2)}, u32[]{:S(2)}) collective-permute-start(bf16[4,128,384]{2,1,0:T(8,128)(2,1)S(1)} %get-tuple-element.144), channel_id=1, source_target_pairs={{0,32},{32,0},{64,96},{96,64},{1,33},{33,1},{65,97},{97,65},{2,34}... | collective-permute-start | bytes 1179656 | tf_op jit(solution)/shard_map/ppermute | solution.py:32
  443.1 18.9 %collective-permute-start.85 = (bf16[128,384]{1,0:T(8,128)(2,1)S(1)}, bf16[128,384]{1,0:T(8,128)(2,1)S(1)}, u32[]{:S(2)}, u32[]{:S(2)}) collective-permute-start(bf16[128,384]{1,0:T(8,128)(2,1)S(1)} %get-tuple-element.224), channel_id=1, source_target_pairs={{0,96},{32,64},{64,32},{96,0},{1,97},{33,65},{65,33},{97,1},{2,98}... | collective-permute-start | bytes 294920 | tf_op jit(solution)/shard_map/ppermute | solution.py:32
  444.1 17.9 %collective-permute-start.84 = (bf16[128,384]{1,0:T(8,128)(2,1)S(1)}, bf16[128,384]{1,0:T(8,128)(2,1)S(1)}, u32[]{:S(2)}, u32[]{:S(2)}) collective-permute-start(bf16[128,384]{1,0:T(8,128)(2,1)S(1)} %get-tuple-element.225), channel_id=1, source_target_pairs={{0,64},{32,96},{64,0},{96,32},{1,65},{33,97},{65,1},{97,33},{2,66}... | collective-permute-start | bytes 294920 | tf_op jit(solution)/shard_map/ppermute | solution.py:32
  474.0 20.1 %collective-permute-start.72 = (bf16[128,2048]{1,0:T(8,128)(2,1)S(1)}, bf16[128,2048]{1,0:T(8,128)(2,1)S(1)}, u32[]{:S(2)}, u32[]{:S(2)}) collective-permute-start(bf16[128,2048]{1,0:T(8,128)(2,1)S(1)} %get-tuple-element.134), channel_id=1, source_target_pairs={{0,18},{1,19},{2,16},{3,17},{16,2},{17,3},{18,0},{19,1},{4,22},{5,... | collective-permute-start | bytes 1572872 | tf_op jit(solution)/shard_map/ppermute | solution.py:28
  475.7 18.3 %collective-permute-start.71 = (bf16[128,2048]{1,0:T(8,128)(2,1)S(1)}, bf16[128,2048]{1,0:T(8,128)(2,1)S(1)}, u32[]{:S(2)}, u32[]{:S(2)}) collective-permute-start(bf16[128,2048]{1,0:T(8,128)(2,1)S(1)} %get-tuple-element.132), channel_id=1, source_target_pairs={{0,2},{1,3},{2,0},{3,1},{16,18},{17,19},{18,16},{19,17},{4,6},{5,7... | collective-permute-start | bytes 1572872 | tf_op jit(solution)/shard_map/ppermute | solution.py:28
  (89 other events, 981.1 us)
Sparse Core Ops, SparseCore 0:
  23.2 112.4 all-gather.1
  286.3 93.1 reduce-scatter.1
